TPU v7x, 512 devices: a whole 4x4x16 slice. The times are simulated.
512 devices in a mesh: dp: 32 (over z_lo, x, core), seq: 16 (over y, z_hi).
Axes of the slice: x: 4, y: 4, z: 16 (z_hi: 4, z_lo: 4; z = z_hi * 4 + z_lo), core: 2. Of those that a mesh axis runs over, the one named last changes fastest.
Arguments:
- normed: bfloat16 [32, 2048, 4096], P('dp', 'seq'), may hold values from -6 to 6
- frozen_query_key_value: bfloat16 [32, 2048, 16, 384], P('dp', 'seq'), may hold values from -6 to 6
- frames: int32 [32, 2048], P('dp'), may hold values from 0 to 15, as said below
- adapter_query_key_value_down: bfloat16 [4096, 64], replicated, may hold values from -0.09375 to 0.09375
- adapter_query_key_value_up: bfloat16 [64, 16, 384], P(None, 'seq'), may hold values from -0.75 to 0.75
- adapter_output_down: bfloat16 [16, 128, 64], P('seq'), may hold values from -0.125 to 0.125
- adapter_output_up: bfloat16 [64, 4096], P(None, 'seq'), may hold values from -0.75 to 0.75
- readout: bfloat16 [4096, 128], P('seq'), may hold values from -0.09375 to 0.09375
- frozen_readout_head: bfloat16 [16, 128, 128], P('seq'), may hold values from -0.125 to 0.125
- residual_velocity: bfloat16 [32, 2048, 128], P('dp'), may hold values from -6 to 6
- sampling_velocity: bfloat16 [32, 2048, 128], P('dp'), may hold values from -12 to 12
- sampler_step_noise: bfloat16 [32, 2048, 128], P('dp'), may hold values from -5 to 5
- rewards: float32 [32], replicated, may hold values from -4 to 4
- rollout_group_index: int32 [32], replicated, may hold values from 0 to 7, never falling along the last dimension, each value on 1 to 6 neighbouring positions
- denoising_step_index: int32 [1], replicated, may hold values from 1 to 3
Outputs:
- grad_in: float32 [4096, 64], P(('dp', 'seq'))
- grad_qkv: float32 [64, 16, 384], P('dp', 'seq')
- grad_out_in: float32 [16, 128, 64], P('seq', None, 'dp')
- grad_out: float32 [64, 4096], P('dp', 'seq')
Inputs may be any that keep to these rules, and one draw needn't show every extreme that they name: `rollout_group_index`: rollouts of one group stand next to each other; a group holds 1 to 6 rollouts. `frames`: each rollout's tokens carry every frame number on 128 tokens, in a drawn order.
All inputs are finite; a program needn't handle non-finite values.
Results may differ from a plain program's by a relative error of at most 0.022.
Values may be sent and summed in bfloat16 or wider, within the bound.
No kernel may reach another device: no remote copies, remote signals or barrier semaphores. Data moves between devices by JAX's collectives and lax.ppermute only.
A program may use at most 64 MiB of HBM per device.

v0:
```python
import math

import jax
import jax.numpy as jnp
from jax import lax
from jax.sharding import PartitionSpec as P

STEPS = 10


ADAPTER_SCALE = 1.0
ROPE_BASE = 10000.0
ETA = 0.7
CLIP = 0.05
ADV_FLOOR = 0.5


def rope_tables(frame_row, head_size):
    half_size = head_size // 2
    inverse = ROPE_BASE ** (-jnp.arange(half_size, dtype=jnp.float32) / half_size)
    angles = frame_row.astype(jnp.float32)[:, None] * inverse[None, :]
    return (jnp.cos(angles), jnp.sin(angles))


def rotate(tensor, cosine_table, sine_table, direction):
    half_size = tensor.shape[-1] // 2
    first_half = tensor[..., :half_size]
    second_half = tensor[..., half_size:]
    cosine_rows = cosine_table[:, None, :]
    sine_rows = direction * sine_table[:, None, :]
    return jnp.concatenate(
        [
            first_half * cosine_rows - second_half * sine_rows,
            first_half * sine_rows + second_half * cosine_rows,
        ],
        axis=-1,
    )


def gap_factor(denoising_step_index, total_steps):
    noise_level = 1.0 - denoising_step_index[0].astype(jnp.float32) / total_steps
    step_width = 1.0 / total_steps
    sigma_value = ETA * jnp.sqrt(noise_level / (1.0 - noise_level))
    spread = sigma_value * math.sqrt(step_width)
    drift_coef = sigma_value * sigma_value / (2.0 * noise_level)
    return step_width * (1.0 + drift_coef * (1.0 - noise_level)) / spread


def advantages(rewards, rollout_group_index):
    same_group = (rollout_group_index[:, None] == rollout_group_index[None, :]).astype(jnp.float32)
    group_size = jnp.sum(same_group, axis=1)
    group_mean = jnp.sum(same_group * rewards[None, :], axis=1) / group_size
    centred = rewards[None, :] - group_mean[:, None]
    group_var = jnp.sum(same_group * centred * centred, axis=1) / group_size
    return (rewards - group_mean) / jnp.maximum(jnp.sqrt(group_var), ADV_FLOOR)


def clip_weight(logratio, advantage):
    ratio = jnp.exp(logratio)
    active = jnp.where(advantage >= 0.0, ratio <= 1.0 + CLIP, ratio >= 1.0 - CLIP)
    return jnp.where(active, advantage * ratio, 0.0)


def body(
    normed,
    frozen_query_key_value,
    frames,
    adapter_query_key_value_down,
    adapter_query_key_value_up,
    adapter_output_down,
    adapter_output_up,
    readout,
    frozen_readout_head,
    residual_velocity,
    sampling_velocity,
    sampler_step_noise,
    rewards,
    rollout_group_index,
    denoising_step_index,
):
    seq_count = lax.axis_size("seq")
    tok_rows = normed.shape[1]
    length = tok_rows * seq_count
    local_head_count = adapter_query_key_value_up.shape[1]
    head_size = frozen_readout_head.shape[1]
    channels = frozen_readout_head.shape[2]
    att_scale = 1.0 / math.sqrt(head_size)
    multiplier = gap_factor(denoising_step_index, STEPS)
    advantage = advantages(rewards, rollout_group_index)[lax.axis_index("dp")]
    readout_rows = lax.psum(
        jnp.dot(adapter_output_up, readout, preferred_element_type=jnp.float32), "seq"
    ).astype(jnp.bfloat16)
    down_projected_rows = jnp.dot(
        normed[0], adapter_query_key_value_down, preferred_element_type=jnp.float32
    ).astype(jnp.bfloat16)
    first_head_index = lax.all_to_all(
        frozen_query_key_value, "seq", split_axis=2, concat_axis=1, tiled=True
    )
    down_projection_full = lax.all_gather(down_projected_rows, "seq", axis=0, tiled=True)
    adapter_update = jnp.einsum(
        "il,lgf->igf",
        down_projection_full,
        adapter_query_key_value_up,
        preferred_element_type=jnp.float32,
    )
    query_key_value_single = (
        first_head_index[0].astype(jnp.float32) + ADAPTER_SCALE * adapter_update
    )
    cosine_table, sine_table = rope_tables(frames[0], head_size)
    queries = rotate(query_key_value_single[..., :head_size], cosine_table, sine_table, 1.0).astype(
        jnp.bfloat16
    )
    keys_all = rotate(
        query_key_value_single[..., head_size : 2 * head_size], cosine_table, sine_table, 1.0
    ).astype(jnp.bfloat16)
    values = query_key_value_single[..., 2 * head_size :].astype(jnp.bfloat16)
    block_rows = min(512, length)
    block_count = length // block_rows

    def forward_block(block_index):
        query_block = lax.dynamic_slice_in_dim(queries, block_index * block_rows, block_rows, 0)
        scores = (
            jnp.einsum("bhd,thd->hbt", query_block, keys_all, preferred_element_type=jnp.float32)
            * att_scale
        )
        row_max = jnp.max(scores, axis=2, keepdims=True)
        exp_scores = jnp.exp(scores - row_max)
        soft_weights = (exp_scores / jnp.sum(exp_scores, axis=2, keepdims=True)).astype(
            jnp.bfloat16
        )
        attended = jnp.einsum(
            "hbt,thd->bhd", soft_weights, values, preferred_element_type=jnp.float32
        ).astype(jnp.bfloat16)
        return (soft_weights, attended)

    stored, attended = lax.map(forward_block, jnp.arange(block_count))
    attention_block = attended.reshape(length, local_head_count, head_size)
    vel_total, down_total = lax.psum(
        (
            jnp.einsum(
                "thd,hdc->tc",
                attention_block,
                frozen_readout_head,
                preferred_element_type=jnp.float32,
            ),
            jnp.einsum(
                "nok,okf->nf",
                attention_block,
                adapter_output_down,
                preferred_element_type=jnp.float32,
            ),
        ),
        "seq",
    )
    output_down_rows = down_total.astype(jnp.bfloat16)
    predicted_velocity = (
        residual_velocity[0].astype(jnp.float32)
        + vel_total
        + ADAPTER_SCALE
        * jnp.dot(output_down_rows, readout_rows, preferred_element_type=jnp.float32)
    )
    scaled_gap = multiplier * (predicted_velocity - sampling_velocity[0].astype(jnp.float32))
    noise_float = sampler_step_noise[0].astype(jnp.float32)
    logratio = -jnp.sum(noise_float * scaled_gap + 0.5 * scaled_gap * scaled_gap) / (
        length * channels
    )
    rollout_weight = clip_weight(logratio, advantage)
    velocity_gradient = (-(rollout_weight * multiplier) * (noise_float + scaled_gap)).astype(
        jnp.bfloat16
    )
    output_down_gradient = (
        ADAPTER_SCALE
        * jnp.dot(velocity_gradient, readout_rows.T, preferred_element_type=jnp.float32)
    ).astype(jnp.bfloat16)
    readout_piece = ADAPTER_SCALE * lax.dot_general(
        output_down_rows,
        velocity_gradient,
        (((0,), (0,)), ((), ())),
        preferred_element_type=jnp.float32,
    )
    grad_heads = (
        jnp.einsum(
            "zo,pjo->zpj",
            velocity_gradient,
            frozen_readout_head,
            preferred_element_type=jnp.float32,
        )
        + jnp.einsum(
            "js,bps->jbp",
            output_down_gradient,
            adapter_output_down,
            preferred_element_type=jnp.float32,
        )
    ).astype(jnp.bfloat16)
    out_in_part = jnp.einsum(
        "thd,tr->hdr", attention_block, output_down_gradient, preferred_element_type=jnp.float32
    )
    row_delta = jnp.sum(
        grad_heads.astype(jnp.float32) * attention_block.astype(jnp.float32), axis=2
    )

    def backward_block(carry, block_index):
        key_grad, value_grad = carry
        begin_row = block_index * block_rows
        soft_weights = stored[block_index]
        query_block = lax.dynamic_slice_in_dim(queries, begin_row, block_rows, 0)
        grad_block = lax.dynamic_slice_in_dim(grad_heads, begin_row, block_rows, 0)
        delta_block = lax.dynamic_slice_in_dim(row_delta, begin_row, block_rows, 0)
        prob_grad = jnp.einsum(
            "bhd,thd->hbt", grad_block, values, preferred_element_type=jnp.float32
        )
        score_grad = (
            soft_weights.astype(jnp.float32) * (prob_grad - delta_block.T[:, :, None])
        ).astype(jnp.bfloat16)
        query_grad = (
            jnp.einsum("hbt,thd->bhd", score_grad, keys_all, preferred_element_type=jnp.float32)
            * att_scale
        )
        key_grad = (
            key_grad
            + jnp.einsum(
                "hbt,bhd->thd", score_grad, query_block, preferred_element_type=jnp.float32
            )
            * att_scale
        )
        value_grad = value_grad + jnp.einsum(
            "hbt,bhd->thd", soft_weights, grad_block, preferred_element_type=jnp.float32
        )
        return ((key_grad, value_grad), query_grad)

    zero_grads = jnp.zeros((length, local_head_count, head_size), jnp.float32)
    (key_grad, value_grad), query_grads = lax.scan(
        backward_block, (zero_grads, zero_grads), jnp.arange(block_count)
    )
    query_grad = query_grads.reshape(length, local_head_count, head_size)
    query_key_value_row_gradient = jnp.concatenate(
        [
            rotate(query_grad, cosine_table, sine_table, -1.0),
            rotate(key_grad, cosine_table, sine_table, -1.0),
            value_grad,
        ],
        axis=-1,
    ).astype(jnp.bfloat16)
    query_key_value_gradient = ADAPTER_SCALE * jnp.einsum(
        "jm,jba->mba",
        down_projection_full,
        query_key_value_row_gradient,
        preferred_element_type=jnp.float32,
    )
    down_gradient = lax.psum_scatter(
        ADAPTER_SCALE
        * jnp.einsum(
            "wiq,diq->wd",
            query_key_value_row_gradient,
            adapter_query_key_value_up,
            preferred_element_type=jnp.float32,
        ),
        "seq",
        scatter_dimension=0,
        tiled=True,
    ).astype(jnp.bfloat16)
    in_partial = lax.dot_general(
        normed[0], down_gradient, (((0,), (0,)), ((), ())), preferred_element_type=jnp.float32
    )
    qkv_total, out_in_total, fold_total = (
        lax.psum_scatter(query_key_value_gradient, "dp", scatter_dimension=0, tiled=True),
        lax.psum_scatter(out_in_part, "dp", scatter_dimension=2, tiled=True),
        lax.psum_scatter(readout_piece, "dp", scatter_dimension=0, tiled=True),
    )
    grad_in = lax.psum_scatter(in_partial, ("dp", "seq"), scatter_dimension=0, tiled=True)
    grad_out = jnp.dot(fold_total, readout.astype(jnp.float32).T, precision=lax.Precision.HIGHEST)
    return (grad_in, qkv_total, out_in_total, grad_out)


def solution(mesh):
    in_specs = (
        P("dp", "seq", None),
        P("dp", "seq", None, None),
        P("dp", None),
        P(),
        P(None, "seq", None),
        P("seq", None, None),
        P(None, "seq"),
        P("seq", None),
        P("seq", None, None),
        P("dp", None, None),
        P("dp", None, None),
        P("dp", None, None),
        P(),
        P(),
        P(),
    )
    out_specs = (P(("dp", "seq"), None), P("dp", "seq", None), P("seq", None, "dp"), P("dp", "seq"))
    return jax.shard_map(body, mesh=mesh, in_specs=in_specs, out_specs=out_specs, check_vma=False)
```

profile of v0, /device:TPU:1, one launch (start us, length us, event | category | flops | bytes accessed | tf_op | source)
XLA Modules:
  0.0 1619.2 jit_solution(16668998792702315882)
XLA Ops:
  7.2 3.1 copy.56
  10.3 18.6 %all-to-all-start = ((bf16[1,128,16,384]{3,1,0,2:T(8,128)(2,1)}), bf16[1,128,16,384]{3,1,0,2:T(8,128)(2,1)}, u32[]{:S(2)}, u32[]{:S(2)}) async-start(bf16[1,128,16,384]{3,1,0,2:T(8,128)(2,1)} %copy.56), calls=%async_computation | async-start | bytes 3145728 | tf_op jit(solution)/shard_map/all_to_all | solution.py:96
  29.7 111.1 %all_gather.3 = bf16[2048,64]{0,1:T(8,128)(2,1)S(1)} all-gather(bf16[128,64]{0,1:T(8,128)(2,1)S(1)} %convolution_convert_fusion.2), channel_id=1, replica_groups=mesh['dp'=32,'seq'=16] {'seq'}, dimensions={0}, use_global_device_ids=true | all-gather | bytes 278528 | tf_op jit(solution)/shard_map/all_gather | solution.py:99
  141.6 3.5 bitcast_convert_fusion
  145.0 3.6 copy.69
  148.6 2.5 add_bitcast_fusion
  157.2 27.5 %while.27 = (s32[]{:T(128)}, bf16[4,1,512,2048]{3,2,1,0:T(8,128)(2,1)}, bf16[4,512,1,128]{3,1,2,0:T(8,128)(2,1)S(1)}, s32[4]{0:T(128)S(1)}, bf16[2048,1,128]{2,0...) while((s32[]{:T(128)}, ...), condition=%wide.region_3.0_spmd, body=%wide.region_0.3_spmd.sunk | while | flops 546372608 | bytes 20196016 | solution.py:136
  190.6 121.5 %all-reduce.19 = (bf16[2048,64]{0,1:T(8,128)(2,1)S(1)}, bf16[64,128]{1,0:T(8,128)(2,1)}) all-reduce(f32[2048,64]{0,1:T(8,128)} %fusion.88, f32[64,128]{1,0:T(8,128)} %fusion.95), channel_id=1, replica_groups=mesh['dp'=32,'seq'=16] {'seq'}, use_global_device_ids=true, to_apply=%region_8.9 | all-reduce | flops 139264 | bytes 835584 | tf_op jit(solution)/shard_map/psum | solution.py:138
  312.1 106.7 %all-reduce.12.cloned.1.call-done = f32[2048,128]{1,0:T(8,128)} async-done(((f32[2048,128]{1,0:T(8,128)}), f32[2048,128]{1,0:T(8,128)}) %all-reduce.12.cloned.1.call-update) | async-done | bytes 1048592 | tf_op jit(solution)/shard_map/psum | solution.py:138
  418.8 3.7 fusion.31
  428.6 58.7 %while.28 = (s32[]{:T(128)}, f32[2048,1,128]{0,2,1:T(8,128)}, f32[2048,1,128]{0,2,1:T(8,128)}, f32[4,512,1,128]{3,1,2,0:T(8,128)}, s32[4]{0:T(128)S(1)}, /*index...) while((s32[]{:T(128)}, f32[2048,1,128]{0,2,1:T(8,128)}, ...), condition=%wide.region_13.14_spmd.clone, body=%wide.region_12.13_spmd.clone.sunk | while | flops 1079312384 | bytes 24845244 | solution.py:232
  431.9 2.7 multiply_convert_fusion.2
  434.6 2.5 fusion.147
  437.1 2.5 fusion.149
  439.5 3.2 fusion.148
  446.1 2.7 multiply_convert_fusion.2
  448.8 2.8 fusion.147
  451.7 2.5 fusion.149
  454.1 3.4 fusion.148
  461.0 2.7 multiply_convert_fusion.2
  463.7 2.8 fusion.147
  466.5 2.4 fusion.149
  469.0 3.4 fusion.148
  475.8 2.7 multiply_convert_fusion.2
  478.5 2.8 fusion.147
  483.8 3.4 fusion.148
  487.3 3.2 fusion.94
  508.3 2.6 convolution_bitcast_fusion.2
  511.1 114.5 %reduce-scatter.5.cloned.1.call-done = f32[128,64]{0,1:T(8,128)} async-done(((f32[2048,64]{0,1:T(8,128)}), f32[128,64]{0,1:T(8,128)}) %reduce-scatter.5.cloned.1.call-update) | async-done | bytes 32784 | tf_op jit(solution)/shard_map/reduce_scatter | solution.py:250
  629.6 247.9 %all-reduce.18.cloned.1.call-done = (f32[1,128,64]{1,2,0:T(8,128)}, f32[64,128]{1,0:T(8,128)}) async-done(((f32[1,128,64]{1,2,0:T(8,128)}, f32[64,128]{1,0:T(8,128)}), (f32[1,128,64]{1,2,0:T(8,128)}, f32[64,128]{1,0:T(8,128)})) %all-reduce.18.cloned.1.call-update) | async-done | bytes 65552
  880.2 257.7 %all-reduce.16.cloned.1.call-done = f32[64,1,384]{2,0,1:T(8,128)} async-done(((f32[64,1,384]{2,0,1:T(8,128)}), f32[64,1,384]{2,0,1:T(8,128)}) %all-reduce.16.cloned.1.call-update) | async-done | bytes 98320
  1139.1 472.1 %all-reduce.14.cloned.1.call-done = f32[4096,64]{0,1:T(8,128)} async-done(((f32[4096,64]{0,1:T(8,128)}), f32[4096,64]{0,1:T(8,128)}) %all-reduce.14.cloned.1.call-update) | async-done | bytes 1048592
  (179 shorter events, 73.2 us)
Async XLA Ops:
  7.2 22.1 %copy-start = (bf16[1,128,4096]{2,1,0:T(8,128)(2,1)S(1)}, bf16[1,128,4096]{2,1,0:T(8,128)(2,1)}, u32[]{:S(2)}) copy-start(bf16[1,128,4096]{2,1,0:T(8,128)(2,1)} %param.19) | copy-start | bytes 3145732
  7.2 21.8 %copy-start.25 = (s32[1,2048]{1,0:T(1,128)S(1)}, s32[1,2048]{1,0:T(1,128)}, u32[]{:S(2)}) copy-start(s32[1,2048]{1,0:T(1,128)} %param.21) | copy-start | bytes 24580
  7.2 21.8 %copy-start.27 = (f32[32]{0:T(128)S(1)}, f32[32]{0:T(128)}, u32[]{:S(2)}) copy-start(f32[32]{0:T(128)} %param.31) | copy-start | bytes 388
  7.2 21.8 %copy-start.26 = (s32[32]{0:T(128)S(1)}, s32[32]{0:T(128)}, u32[]{:S(2)}) copy-start(s32[32]{0:T(128)} %param.32) | copy-start | bytes 388
  7.2 22.0 %copy-start.17 = (bf16[4096,64]{0,1:T(8,128)(2,1)S(1)}, bf16[4096,64]{0,1:T(8,128)(2,1)}, u32[]{:S(2)}) copy-start(bf16[4096,64]{0,1:T(8,128)(2,1)} %param.22) | copy-start | bytes 1572868
  10.3 130.5 %copy-start.18 = (bf16[256,128]{1,0:T(8,128)(2,1)S(1)}, bf16[256,128]{1,0:T(8,128)(2,1)}, u32[]{:S(2)}) copy-start(bf16[256,128]{1,0:T(8,128)(2,1)} %param.26) | copy-start | bytes 196612
  10.3 130.5 %copy-start.24 = (bf16[64,256]{1,0:T(8,128)(2,1)S(1)}, bf16[64,256]{1,0:T(8,128)(2,1)}, u32[]{:S(2)}) copy-start(bf16[64,256]{1,0:T(8,128)(2,1)} %param.25) | copy-start | bytes 98308
  10.3 131.2 %all-to-all-start = ((bf16[1,128,16,384]{3,1,0,2:T(8,128)(2,1)}), bf16[1,128,16,384]{3,1,0,2:T(8,128)(2,1)}, u32[]{:S(2)}, u32[]{:S(2)}) async-start(bf16[1,128,16,384]{3,1,0,2:T(8,128)(2,1)} %copy.56), calls=%async_computation | async-start | bytes 3145728 | tf_op jit(solution)/shard_map/all_to_all | solution.py:96
  28.9 389.9 %all-reduce.12.cloned.1.call-start = ((), (), s32[]{:S(2)}) async-start(), calls=%async_computation.2 | async-start | bytes 2097152 | tf_op jit(solution)/shard_map/psum | solution.py:138
  140.8 7.8 copy-start.11
  145.0 3.6 copy-start.19
  157.2 27.6 %copy-start.20 = (bf16[1,128,128]{2,1,0:T(8,128)(2,1)S(1)}, bf16[1,128,128]{2,1,0:T(8,128)(2,1)}, u32[]{:S(2)}) copy-start(bf16[1,128,128]{2,1,0:T(8,128)(2,1)} %param.27) | copy-start | bytes 98308
  184.8 237.7 %copy-start.6 = (bf16[4,512,1,128]{3,1,2,0:T(8,128)(2,1)}, bf16[4,512,1,128]{3,1,2,0:T(8,128)(2,1)S(1)}, u32[]{:S(2)}) copy-start(bf16[4,512,1,128]{3,1,2,0:T(8,128)(2,1)S(1)} %get-tuple-element.102) | copy-start | bytes 1572868
  184.8 4.7 copy-start.21
  184.8 234.0 %copy-start.13 = (bf16[1,2048,128]{2,1,0:T(8,128)(2,1)S(1)}, bf16[1,2048,128]{2,1,0:T(8,128)(2,1)}, u32[]{:S(2)}) copy-start(bf16[1,2048,128]{2,1,0:T(8,128)(2,1)} %param.30) | copy-start | bytes 1572868
  186.1 439.5 %reduce-scatter.5.cloned.1.call-start = ((), (), s32[]{:S(2)}) async-start(), calls=%async_computation.3 | async-start | bytes 557056 | tf_op jit(solution)/shard_map/reduce_scatter | solution.py:250
  312.1 111.8 %copy-start.15 = (bf16[2048,64]{0,1:T(8,128)(2,1)}, bf16[2048,64]{0,1:T(8,128)(2,1)S(1)}, u32[]{:S(2)}) copy-start(bf16[2048,64]{0,1:T(8,128)(2,1)S(1)} %get-tuple-element.270) | copy-start | bytes 786436
  422.5 4.9 copy-start.14
  454.1 3.5 copy-start.2
  454.1 3.5 copy-start.10
  454.1 3.5 copy-start.23
  469.0 3.5 copy-start.2
  469.0 3.5 copy-start.10
  469.0 3.5 copy-start.23
  490.5 7.7 copy-start.3
  498.2 8.4 copy-start.7
  500.5 6.9 copy-start.5
  502.8 4.7 copy-start.16
  502.8 5.6 copy-start.12
  506.5 370.9 %all-reduce.18.cloned.1.call-start = ((), (), s32[]{:S(2)}) async-start(), calls=%async_computation.6 | async-start | bytes 131072
  508.3 629.5 %all-reduce.16.cloned.1.call-start = ((), (), s32[]{:S(2)}) async-start(), calls=%async_computation.5 | async-start | bytes 196608
  511.0 1100.2 %all-reduce.14.cloned.1.call-start = ((), (), s32[]{:S(2)}) async-start(), calls=%async_computation.4 | async-start | bytes 2097152
  (20 other events, 62.2 us)
Sparse Core Ops, SparseCore 0:
  186.2 232.4 all-reduce.11
  506.7 118.8 reduce-scatter.4
  628.6 248.8 all-reduce.17
  880.5 257.2 all-reduce.15
  1143.1 468.0 all-reduce.13
where the time goes:
time: 1620 us
  waiting for transfers between devices  1200 us (74%)
  blocking collectives  233 us (14%)
  matrix products  77.5 us (5%)
  other arithmetic  31.1 us (2%)
  local copies, waits for them, and re-layouts  29.2 us (2%)
  starting transfers between devices  18.8 us (1%)
  between operations  17.8 us (1%)
    unnamed x8, waiting for transfers between devices  978 us
    psum x1, blocking collectives, body(): lax.psum((jnp.einsum('thd,hdc->tc', attention_block, frozen_readout_head,...  121 us
    reduce_scatter x1, waiting for transfers between devices, body(): lax.psum_scatter(ADAPTER_SCALE * jnp.einsum('wiq,diq->wd', query_key_valu...  115 us
    all_gather x1, blocking collectives, body(): lax.all_gather(down_projected_rows, 'seq', axis=0, tiled=True)  111 us
    psum x1, waiting for transfers between devices, body(): lax.psum((jnp.einsum('thd,hdc->tc', attention_block, frozen_readout_head,...  107 us
  transfers between devices with their start and end apart: 6, of which 5 were waited for; matrix products, arithmetic and copies ran while one was open for 1% of the time, Pallas kernels for 0%

commit v1 on v0

v1 whole, which is shorter than its diff:
```python
import functools
import math

import jax
import jax.numpy as jnp
from jax import lax
from jax.experimental import pallas as pl
from jax.experimental.pallas import tpu as pltpu
from jax.sharding import Mesh
from jax.sharding import PartitionSpec as P

STEPS = 10
ROPE_BASE = 10000.0
ETA = 0.7
CLIP = 0.05
ADV_FLOOR = 0.5

NAMES = ("zlo", "x", "core", "y", "zhi")
SIZES = (4, 4, 2, 4, 4)
DP = ("zlo", "x", "core")
SEQ = ("y", "zhi")
XC = ("x", "core")
Z = ("zlo", "zhi")

HEADS = 4
TOK = 128
OWN = 512
LENGTH = 2048
HD = 128
RANK = 64
SCALE = 1.0 / math.sqrt(HD)
F32 = jnp.float32
BF16 = jnp.bfloat16
VMEM_LIMIT = 56 * 1024 * 1024


def exchange(pieces, axes):
    return lax.all_to_all(pieces, axes, split_axis=0, concat_axis=0, tiled=True)


def spread(value, axes, count):
    return exchange(jnp.broadcast_to(value[None], (count,) + value.shape), axes)


def dot(a, b, dims=(1, 0)):
    return lax.dot_general(a, b, (((dims[0],), (dims[1],)), ((), ())), preferred_element_type=F32)


def gap_factor(denoising_step_index):
    noise_level = 1.0 - denoising_step_index[0].astype(F32) / STEPS
    step_width = 1.0 / STEPS
    sigma_value = ETA * jnp.sqrt(noise_level / (1.0 - noise_level))
    spread_value = sigma_value * math.sqrt(step_width)
    drift_coef = sigma_value * sigma_value / (2.0 * noise_level)
    return step_width * (1.0 + drift_coef * (1.0 - noise_level)) / spread_value


def advantages(rewards, rollout_group_index):
    same_group = (rollout_group_index[:, None] == rollout_group_index[None, :]).astype(F32)
    group_size = jnp.sum(same_group, axis=1)
    group_mean = jnp.sum(same_group * rewards[None, :], axis=1) / group_size
    centred = rewards[None, :] - group_mean[:, None]
    group_var = jnp.sum(same_group * centred * centred, axis=1) / group_size
    return (rewards - group_mean) / jnp.maximum(jnp.sqrt(group_var), ADV_FLOOR)


def clip_weight(logratio, advantage):
    ratio = jnp.exp(logratio)
    active = jnp.where(advantage >= 0.0, ratio <= 1.0 + CLIP, ratio >= 1.0 - CLIP)
    return jnp.where(active, advantage * ratio, 0.0)


def rope_tables(frame_row):
    half = HD // 2
    inverse = ROPE_BASE ** (-jnp.arange(half, dtype=F32) / half)
    angles = frame_row.astype(F32)[:, None] * inverse[None, :]
    cos, sin = jnp.cos(angles), jnp.sin(angles)
    return jnp.concatenate([cos, cos], axis=1), jnp.concatenate([-sin, sin], axis=1)


def swap_halves(tensor):
    half = HD // 2
    return jnp.concatenate([tensor[..., half:], tensor[..., :half]], axis=-1)


def forward_kernel(q_ref, k_ref, v_ref, rh_ref, ad_ref, folded_ref, att_ref, prob_ref, inv_ref, vel_ref, od_ref, vel_acc, od_acc):
    head = pl.program_id(0)
    scores = dot(k_ref[0], q_ref[0], (1, 1))
    peak = jnp.max(scores, axis=0, keepdims=True)
    weights = jnp.exp((scores - peak) * SCALE)
    inverse = 1.0 / jnp.sum(weights, axis=0, keepdims=True)
    weights = weights.astype(BF16)
    prob_ref[0] = weights
    inv_ref[0] = inverse
    attended = dot(v_ref[0], weights, (0, 0)) * inverse
    att = attended.T.astype(BF16)
    att_ref[0] = att
    velocity = dot(att, rh_ref[0])
    down = dot(att, ad_ref[0])

    @pl.when(head == 0)
    def _():
        vel_acc[...] = velocity
        od_acc[...] = down

    @pl.when(head > 0)
    def _():
        vel_acc[...] += velocity
        od_acc[...] += down

    @pl.when(head == HEADS - 1)
    def _():
        out_down = od_acc[...].astype(BF16)
        od_ref[...] = out_down
        vel_ref[...] = (vel_acc[...] + dot(out_down, folded_ref[...])).astype(BF16)


def forward(q, k, v, rh, ad, folded):
    per_head = lambda *dims: pl.BlockSpec((1,) + dims, lambda h: (h,) + (0,) * len(dims))
    whole = lambda *dims: pl.BlockSpec(dims, lambda h: (0,) * len(dims))
    return pl.pallas_call(
        forward_kernel,
        grid=(HEADS,),
        in_specs=[
            per_head(OWN, HD),
            per_head(LENGTH, HD),
            per_head(LENGTH, HD),
            per_head(HD, HD),
            per_head(HD, RANK),
            whole(RANK, HD),
        ],
        out_specs=[
            per_head(OWN, HD),
            per_head(LENGTH, OWN),
            per_head(1, OWN),
            whole(OWN, HD),
            whole(OWN, RANK),
        ],
        out_shape=[
            jax.ShapeDtypeStruct((HEADS, OWN, HD), BF16),
            jax.ShapeDtypeStruct((HEADS, LENGTH, OWN), BF16),
            jax.ShapeDtypeStruct((HEADS, 1, OWN), F32),
            jax.ShapeDtypeStruct((OWN, HD), BF16),
            jax.ShapeDtypeStruct((OWN, RANK), BF16),
        ],
        scratch_shapes=[pltpu.VMEM((OWN, HD), F32), pltpu.VMEM((OWN, RANK), F32)],
        compiler_params=pltpu.CompilerParams(vmem_limit_bytes=VMEM_LIMIT),
        name="attention_forward",
    )(q, k, v, rh, ad, folded)


def unrotate(grad, cos, sin):
    return (grad * cos - pltpu.roll(grad, HD // 2, 1) * sin).astype(BF16)


def backward_kernel(
    y_ref, q_ref, k_ref, v_ref, prob_ref, inv_ref, att_ref, g_ref, og_ref, rh_ref, ad_ref, up_ref,
    down_ref, own_ref, cos_ref, sin_ref, cos_own_ref, sin_own_ref, dgrad_ref, qkv_ref, oi_ref, dg_acc, own_acc,
):
    head = pl.program_id(0)
    att = att_ref[0]
    og = og_ref[...]
    att_grad = (dot(g_ref[...], rh_ref[0], (1, 1)) + dot(og, ad_ref[0], (1, 1))).astype(BF16)
    att_grad = att_grad.astype(F32)
    inverse = inv_ref[0]
    delta = jnp.sum((att_grad * att.astype(F32)).T, axis=0, keepdims=True) * inverse
    scaled = (att_grad * jnp.broadcast_to(inverse, (HD, OWN)).T).astype(BF16)
    weights = prob_ref[0]
    prob_grad = dot(v_ref[0], scaled, (1, 1))
    score_grad = (weights.astype(F32) * (prob_grad - delta)).astype(BF16)
    v_grad = dot(weights, scaled).astype(BF16)
    k_grad = unrotate(dot(score_grad, q_ref[0]) * SCALE, cos_ref[...], sin_ref[...])
    q_grad = dot(k_ref[0], score_grad, (0, 0)) * SCALE
    q_grad = unrotate(q_grad.T, cos_own_ref[...], sin_own_ref[...])
    up = up_ref[0]
    share = dot(k_grad, up[:, HD : 2 * HD], (1, 1)) + dot(v_grad, up[:, 2 * HD :], (1, 1))

    q_share = dot(q_grad, up[:, :HD], (1, 1))

    @pl.when(head == 0)
    def _():
        dg_acc[...] = share
        own_acc[...] = q_share

    @pl.when(head > 0)
    def _():
        dg_acc[...] += share
        own_acc[...] += q_share

    qkv_ref[0, :, :HD] = dot(own_ref[...], q_grad, (0, 0)).astype(BF16)
    qkv_ref[0, :, HD : 2 * HD] = dot(down_ref[...], k_grad, (0, 0)).astype(BF16)
    qkv_ref[0, :, 2 * HD :] = dot(down_ref[...], v_grad, (0, 0)).astype(BF16)
    oi_ref[0] = dot(og, att, (0, 0)).astype(BF16)

    @pl.when(head == HEADS - 1)
    def _():
        dgrad_ref[...] = dg_acc[...].astype(BF16)
        mine = pl.ds(pl.multiple_of(y_ref[0] * OWN, OWN), OWN)
        dgrad_ref[mine, :] = (dg_acc[mine, :] + own_acc[...]).astype(BF16)


def backward(y, q, k, v, prob, inv, att, g, og, rh, ad, up, down, own, cos, sin, cos_own, sin_own):
    per_head = lambda *dims: pl.BlockSpec((1,) + dims, lambda h: (h,) + (0,) * len(dims))
    whole = lambda *dims: pl.BlockSpec(dims, lambda h: (0,) * len(dims))
    return pl.pallas_call(
        backward_kernel,
        grid=(HEADS,),
        in_specs=[
            pl.BlockSpec(memory_space=pltpu.SMEM),
            per_head(OWN, HD),
            per_head(LENGTH, HD),
            per_head(LENGTH, HD),
            per_head(LENGTH, OWN),
            per_head(1, OWN),
            per_head(OWN, HD),
            whole(OWN, HD),
            whole(OWN, RANK),
            per_head(HD, HD),
            per_head(HD, RANK),
            per_head(RANK, 3 * HD),
            whole(LENGTH, RANK),
            whole(OWN, RANK),
            whole(LENGTH, HD),
            whole(LENGTH, HD),
            whole(OWN, HD),
            whole(OWN, HD),
        ],
        out_specs=[whole(LENGTH, RANK), per_head(RANK, 3 * HD), per_head(RANK, HD)],
        out_shape=[
            jax.ShapeDtypeStruct((LENGTH, RANK), BF16),
            jax.ShapeDtypeStruct((HEADS, RANK, 3 * HD), BF16),
            jax.ShapeDtypeStruct((HEADS, RANK, HD), BF16),
        ],
        scratch_shapes=[pltpu.VMEM((LENGTH, RANK), F32), pltpu.VMEM((OWN, RANK), F32)],
        compiler_params=pltpu.CompilerParams(vmem_limit_bytes=VMEM_LIMIT),
        name="attention_backward",
    )(y, q, k, v, prob, inv, att, g, og, rh, ad, up, down, own, cos, sin, cos_own, sin_own)


def fold_lanes(rows):
    n = rows.shape[0] // 2
    return jnp.concatenate([rows[:n], rows[n:]], axis=1)


def unfold_lanes(rows):
    return jnp.concatenate([rows[..., :64], rows[..., 64:]], axis=-2)


def body(
    normed,
    frozen,
    frames,
    qkv_down,
    qkv_up,
    out_down_adapter,
    out_up,
    readout,
    readout_head,
    residual_velocity,
    sampling_velocity,
    sampler_step_noise,
    rewards,
    rollout_group_index,
    denoising_step_index,
):
    y = lax.axis_index("y")
    zhi = lax.axis_index("zhi")
    multiplier = gap_factor(denoising_step_index)
    advantage = advantages(rewards, rollout_group_index)[lax.axis_index(DP)]

    pack = jnp.concatenate(
        [qkv_up[:, 0, :HD], qkv_up[:, 0, HD : 2 * HD], qkv_up[:, 0, 2 * HD :], out_down_adapter[0].T, readout_head[0]]
    )
    pack = spread(pack, "y", 4)
    up = jnp.concatenate([pack[:, :64], pack[:, 64:128], pack[:, 128:192]], axis=2)
    ad = jnp.swapaxes(pack[:, 192:256], 1, 2)
    rh = pack[:, 256:]

    down_rows = dot(normed[0], qkv_down).astype(BF16)
    fold_part = dot(out_up, readout).astype(BF16)
    parts = frozen[0].reshape(TOK, 4, 4, 3, HD).transpose(2, 3, 1, 0, 4)
    extra = jnp.concatenate([fold_lanes(down_rows), fold_part])
    extra = jnp.broadcast_to(extra[None], (4,) + extra.shape)
    send_kv = jnp.concatenate([parts[:, 1:].reshape(4, 8 * TOK, HD), extra], axis=1)
    send_q = parts[:, 0].reshape(4, 4 * TOK, HD)
    got_kv = exchange(send_kv, "zhi")
    got_q = exchange(send_q, "zhi")

    down_own = unfold_lanes(got_kv[:, 8 * TOK : 8 * TOK + 64]).reshape(OWN, RANK)
    fold_z = jnp.sum(got_kv[:, 8 * TOK + 64 :].astype(F32), axis=0).astype(BF16)
    cos, sin = rope_tables(frames[0])
    cos_own = lax.dynamic_slice_in_dim(cos, y * OWN, OWN, 0)
    sin_own = lax.dynamic_slice_in_dim(sin, y * OWN, OWN, 0)
    update = jnp.einsum("tr,hrd->htd", down_own, up, preferred_element_type=F32)

    def tokens(block):
        return block.reshape(4, 4, TOK, HD).swapaxes(0, 1).reshape(4, OWN, HD).astype(F32)

    def rotated(tensor):
        return (tensor * cos_own + swap_halves(tensor) * sin_own).astype(BF16)

    k_own = rotated(tokens(got_kv[:, : 4 * TOK]) + update[..., HD : 2 * HD])
    v_own = (tokens(got_kv[:, 4 * TOK : 8 * TOK]) + update[..., 2 * HD :]).astype(BF16)
    shared = jnp.concatenate(
        [k_own.reshape(4 * OWN, HD), v_own.reshape(4 * OWN, HD), fold_lanes(down_own), fold_z]
    )
    shared = lax.all_gather(shared, "y", axis=0, tiled=False)
    k = shared[:, : 4 * OWN].reshape(4, 4, OWN, HD).swapaxes(0, 1).reshape(4, LENGTH, HD)
    v = shared[:, 4 * OWN : 8 * OWN].reshape(4, 4, OWN, HD).swapaxes(0, 1).reshape(4, LENGTH, HD)
    down_all = unfold_lanes(shared[:, 8 * OWN : 8 * OWN + 256]).reshape(LENGTH, RANK)
    folded = jnp.sum(shared[:, 8 * OWN + 256 :].astype(F32), axis=0).astype(BF16)
    q = rotated(tokens(got_q) + update[..., :HD])

    att, prob, inv, vel_part, out_down = forward(q, k, v, rh, ad, folded)

    velocity = jnp.sum(spread(vel_part, "zhi", 4).astype(F32), axis=0)
    own = lambda array: lax.dynamic_slice_in_dim(array[0], y * OWN, OWN, 0).astype(F32)
    gap = multiplier * (own(residual_velocity) + velocity - own(sampling_velocity))
    noise = own(sampler_step_noise)
    log_part = -jnp.sum(noise * gap + 0.5 * gap * gap) / (LENGTH * HD)
    g = (noise + gap).astype(BF16)
    og = dot(g, folded, (1, 1)).astype(BF16)
    fold_grad = dot(out_down, g, (0, 0)).astype(BF16)

    down_grad, qkv_grad, oi_grad = backward(
        y[None].astype(jnp.int32), q, k, v, prob, inv, att, g, og, rh, ad, up, down_all, down_own, cos, sin, cos_own, sin_own
    )

    high = lax.reduce_precision(log_part, 8, 7)
    middle = lax.reduce_precision(log_part - high, 8, 7)
    low = lax.reduce_precision(log_part - high - middle, 8, 7)
    lane = lax.broadcasted_iota(jnp.int32, (16, HD), 1)
    log_rows = jnp.where(lane == 0, high, jnp.where(lane == 1, middle, jnp.where(lane == 2, low, 0.0)))
    send = jnp.concatenate(
        [
            jnp.stack([fold_lanes(b) for b in down_grad.reshape(4, OWN, RANK)]),
            qkv_grad[:, :, :HD],
            qkv_grad[:, :, HD : 2 * HD],
            qkv_grad[:, :, 2 * HD :],
            oi_grad,
            jnp.broadcast_to(fold_grad[None], (4, RANK, HD)),
            jnp.broadcast_to(log_rows.astype(BF16)[None], (4, 16, HD)),
        ],
        axis=1,
    )
    got = exchange(send, "y").astype(F32)
    total = jnp.sum(got, axis=0)
    logratio = jnp.sum(total[576, :3])
    weight = -(clip_weight(logratio, advantage) * multiplier)
    small = jnp.concatenate([total[256 + 64 * i : 320 + 64 * i] for i in range(5)], axis=1) * weight
    down_z = (unfold_lanes(total[:256]) * weight).astype(BF16)

    down_z = jnp.stack([fold_lanes(b) for b in down_z.reshape(4, TOK, RANK)])
    down_z = jnp.sum(exchange(down_z, "zhi").astype(F32), axis=0)
    down_z = unfold_lanes(down_z).astype(BF16)
    halves = [dot(normed[0][:, half * 2048 : half * 2048 + 2048], down_z, (0, 0)) for half in range(2)]
    in_part = jnp.concatenate(halves, axis=1).astype(BF16)
    in_part = in_part.reshape(16, 4, 32, 128).swapaxes(0, 1).reshape(4, 512, 128)
    in_part = jnp.sum(exchange(in_part, "y").astype(F32), axis=0)

    in_part = in_part.reshape(2, 8, 32, 128).swapaxes(0, 1).reshape(8, 64, 128)
    small = small.reshape(4, 8, 2, 5, HD).transpose(1, 0, 2, 3, 4).reshape(8, 40, HD)
    small = jnp.concatenate([small, jnp.zeros((8, 8, HD), F32)], axis=1)
    both = jnp.concatenate([in_part, small], axis=1).astype(BF16)
    both = jnp.sum(exchange(both, XC).astype(F32), axis=0)
    in_part = both[:64].reshape(2, 4, 8, 2, 64).transpose(3, 0, 1, 2, 4).reshape(4, 4, 4, HD)
    small = both[64:104].reshape(4, 1, 10, HD)
    here = (lax.broadcasted_iota(jnp.int32, (4, 4, 10, HD), 1) == zhi).astype(F32)
    everywhere = lax.broadcasted_iota(jnp.int32, (4, 4, 10, HD), 2) % 5 == 4
    small = small * jnp.where(everywhere, 1.0, here)
    last = jnp.concatenate([in_part, small, jnp.zeros((4, 4, 2, HD), F32)], axis=2).astype(BF16)
    last = jnp.sum(exchange(last.reshape(16, 16, HD), Z).astype(F32), axis=0)
    grad_in = last[:4].reshape(8, 64)
    small = last[4:14].reshape(2, 5, HD)
    grad_qkv = small[:, None, :3].reshape(2, 1, 3 * HD)
    grad_out_in = small[:, 3].T[None]
    grad_out = lax.dot_general(
        small[:, 4], readout.astype(F32), (((1,), (1,)), ((), ())), precision=lax.Precision.HIGHEST
    )
    return grad_in, grad_qkv, grad_out_in, grad_out


def solution(mesh):
    mesh = Mesh(mesh.devices.reshape(SIZES), NAMES)
    in_specs = (
        P(DP, SEQ, None),
        P(DP, SEQ, None, None),
        P(DP, None),
        P(),
        P(None, SEQ, None),
        P(SEQ, None, None),
        P(None, SEQ),
        P(SEQ, None),
        P(SEQ, None, None),
        P(DP, None, None),
        P(DP, None, None),
        P(DP, None, None),
        P(),
        P(),
        P(),
    )
    out_specs = (P(DP + SEQ, None), P(DP, SEQ, None), P(SEQ, None, DP), P(DP, SEQ))
    return jax.shard_map(body, mesh=mesh, in_specs=in_specs, out_specs=out_specs, check_vma=False)
```

time: 1620 us -> 377 us (0.23)
  waiting for transfers between devices: 1200 us -> 179 us
  blocking collectives: 233 us -> 15.2 us
  matrix products: 77.5 us -> 2.74 us
  starting transfers between devices: 18.8 us -> 60.7 us
  Pallas kernels: 0 us -> 33.1 us
    unnamed x8 -> x1, waiting for transfers between devices: 978 us -> 0.02 us
    psum x1 -> x0, blocking collectives: 121 us -> none  [body(): lax.psum((jnp.einsum('thd,hdc->tc', attention_block, frozen_readout_head,...]
    reduce_scatter x1 -> x0, waiting for transfers between devices: 115 us -> none  [body(): lax.psum_scatter(ADAPTER_SCALE * jnp.einsum('wiq,diq->wd', query_key_valu...]
    all_gather x1 -> x0, blocking collectives: 111 us -> none  [body(): lax.all_gather(down_projected_rows, 'seq', axis=0, tiled=True)]
    psum x1 -> x0, waiting for transfers between devices: 107 us -> none  [body(): lax.psum((jnp.einsum('thd,hdc->tc', attention_block, frozen_readout_head,...]
    all_to_all x1 -> x8, waiting for transfers between devices: 0.01 us -> 98.4 us  [exchange(): return lax.all_to_all(pieces, axes, split_axis=0, concat_axis=0, tiled=True)]
    all_gather x0 -> x1, waiting for transfers between devices: none -> 80.4 us  [body(): shared = lax.all_gather(shared, 'y', axis=0, tiled=False)]
    dot_general x39 -> x8, matrix products: 77.5 us -> 2.74 us  [the longest x6 1.43 us: dot(): lax.dot_general(a, b, (((dims[0],), (dims[1],)), ((), ())), preferred_ele...]
  transfers between devices with their start and end apart: 6 -> 9, of which waited for: 5 -> 9; matrix products, arithmetic and copies ran while one was open for 1% -> 6% of each run, Pallas kernels for 0% -> 0%
where the time goes in v1:
time: 377 us; the launch traced here: 375 us
  waiting for transfers between devices  179 us (47%)
  starting transfers between devices  60.7 us (16%)
  local copies, waits for them, and re-layouts  38.4 us (10%)
  Pallas kernels  33.1 us (9%)
  other arithmetic  25.4 us (7%)
  between operations  21.1 us (6%)
  blocking collectives  15.2 us (4%)
    all_to_all x8, waiting for transfers between devices, exchange(): return lax.all_to_all(pieces, axes, split_axis=0, concat_axis=0, tiled=True)  98.4 us
    all_gather x1, waiting for transfers between devices, body(): shared = lax.all_gather(shared, 'y', axis=0, tiled=False)  80.4 us
    all_to_all x8, starting transfers between devices, exchange(): return lax.all_to_all(pieces, axes, split_axis=0, concat_axis=0, tiled=True)  60.7 us
    pallas_call x1, Pallas kernels, backward(): pl.pallas_call(backward_kernel, grid=(HEADS,), in_specs=[pl.BlockSpec(mem...  19.1 us
    all_to_all x1, blocking collectives, exchange(): return lax.all_to_all(pieces, axes, split_axis=0, concat_axis=0, tiled=True)  15.2 us
    pallas_call x1, Pallas kernels, forward(): pl.pallas_call(forward_kernel, grid=(HEADS,), in_specs=[per_head(OWN, HD)...  14.1 us
    unnamed x70, local copies, waits for them, and re-layouts  10.1 us
  transfers between devices with their start and end apart: 9, of which 9 were waited for; matrix products, arithmetic and copies ran while one was open for 6% of the time, Pallas kernels for 0%

profile of v1, /device:TPU:1, one launch (start us, length us, event | category | flops | bytes accessed | tf_op | source)
XLA Modules:
  0.0 375.5 jit_solution(1388513634327437467)
XLA Ops:
  11.7 5.0 %all-to-all-start.1 = ((bf16[4,384,128]{2,1,0:T(8,128)(2,1)}), bf16[4,384,128]{2,1,0:T(8,128)(2,1)S(1)}, u32[]{:S(2)}, u32[]{:S(2)}) async-start(bf16[4,384,128]{2,1,0:T(8,128)(2,1)} %broadcast_in_dim.37), calls=%async_computation.1 | async-start | bytes 786432 | tf_op jit(solution)/shard_map/all_to_all | solution.py:38
  16.7 2.1 copy.94
  19.9 3.1 all-to-all-done.1
  23.7 15.4 %all-to-all-start = ((bf16[4,512,128]{2,1,0:T(8,128)(2,1)}), bf16[4,512,128]{2,1,0:T(8,128)(2,1)}, u32[]{:S(2)}, u32[]{:S(2)}) async-start(bf16[4,512,128]{2,1,0:T(8,128)(2,1)} %bitcast.3), calls=%async_computation | async-start | bytes 1048576 | tf_op jit(solution)/shard_map/all_to_all | solution.py:38
  40.2 1.7 copy.97
  43.7 21.5 %all-to-all-done = bf16[4,512,128]{2,1,0:T(8,128)(2,1)} async-done(((bf16[4,512,128]{2,1,0:T(8,128)(2,1)}), bf16[4,512,128]{2,1,0:T(8,128)(2,1)}, u32[]{:S(2)}, u32[]{:S(2)}) %all-to-all-start) | async-done | bytes 524320 | tf_op jit(solution)/shard_map/all_to_all | solution.py:38
  65.2 6.3 %all-to-all-start.2 = ((bf16[4,1152,128]{2,1,0:T(8,128)(2,1)}), bf16[4,1152,128]{2,1,0:T(8,128)(2,1)}, u32[]{:S(2)}, u32[]{:S(2)}) async-start(bf16[4,1152,128]{2,1,0:T(8,128)(2,1)} %pad_maximum_fusion), calls=%async_computation.2 | async-start | bytes 2359296 | tf_op jit(solution)/shard_map/all_to_all | solution.py:38
  71.6 3.7 multiply_cosine_fusion
  79.2 20.3 %all-to-all-done.2 = bf16[4,1152,128]{2,1,0:T(8,128)(2,1)} async-done(((bf16[4,1152,128]{2,1,0:T(8,128)(2,1)}), bf16[4,1152,128]{2,1,0:T(8,128)(2,1)}, u32[]{:S(2)}, u32[]{:S(2)}) %all-to-all-start.2) | async-done | bytes 1179680 | tf_op jit(solution)/shard_map/all_to_all | solution.py:38
  104.7 1.4 fusion.6
  108.9 1.6 slice.353.rh_ref
  110.4 80.4 %all-gather.3.cloned.1.call-done = bf16[17664,128]{1,0:T(8,128)(2,1)} async-done(((bf16[4416,128]{1,0:T(8,128)(2,1)}), bf16[17664,128]{1,0:T(8,128)(2,1)}) %all-gather.3.cloned.1.call-update) | async-done | bytes 4522000 | tf_op jit(solution)/shard_map/all_gather | solution.py:307
  190.8 1.5 slice_reduce_fusion.folded_ref
  192.3 2.5 fusion.28
  194.8 1.5 copy.103
  196.3 1.5 copy.102
  197.8 14.1 %attention_forward.1 = (bf16[4,512,128]{2,1,0:T(8,128)(2,1)}, bf16[4,2048,512]{2,1,0:T(8,128)(2,1)}, f32[4,1,512]{2,1,0:T(1,128)}, bf16[512,128]{1,0:T(8,128)(2,1)}, bf16[512,64]{1,0:T(8,128)(2,1)}) custom-call(bf16[4,512,128]{2,1,0:T(8,128)(2,1)} %get-tuple-element.64.q_ref, bf16[4,2048,128]{2,1,0:T(8,128)(2,1)} %bitcast.139, ...), custom_call_target="tpu_custom_call" | custom-call | tf_op jit(solution)/shard_map/attention_forward/pallas_call | solution.py:121
  211.9 1.8 broadcast_in_dim.39
  213.6 11.9 %all-to-all-start.3 = ((bf16[4,512,128]{2,1,0:T(8,128)(2,1)}), bf16[4,512,128]{2,1,0:T(8,128)(2,1)}, u32[]{:S(2)}, u32[]{:S(2)}) async-start(bf16[4,512,128]{2,1,0:T(8,128)(2,1)} %broadcast_in_dim.39), calls=%async_computation.3 | async-start | bytes 1048576 | tf_op jit(solution)/shard_map/all_to_all | solution.py:38
  226.4 1.9 pad_maximum_fusion.2
  231.2 23.5 %all-to-all-done.3 = bf16[4,512,128]{2,1,0:T(8,128)(2,1)} async-done(((bf16[4,512,128]{2,1,0:T(8,128)(2,1)}), bf16[4,512,128]{2,1,0:T(8,128)(2,1)}, u32[]{:S(2)}, u32[]{:S(2)}) %all-to-all-start.3) | async-done | bytes 524320 | tf_op jit(solution)/shard_map/all_to_all | solution.py:38
  255.9 1.8 fusion.12
  262.9 19.1 %attention_backward.1 = (bf16[2048,64]{1,0:T(8,128)(2,1)}, bf16[4,64,384]{2,1,0:T(8,128)(2,1)}, bf16[4,64,128]{2,1,0:T(8,128)(2,1)}) custom-call(s32[1]{0:T(128)} %bitcast.y_ref, bf16[4,512,128]{2,1,0:T(8,128)(2,1)} %get-tuple-element.64.q_ref, bf16[4,2048,128]{2,1,0:T(8,128)(2,1)} %bitcast.140, bf16[4,2048,128]{2,1,0:T(8,128)(2,1)} %bitcast.138, ...), custom_call_target="tpu_custom_call" | custom-call | tf_op jit(solution)/shard_map/attention_backward/pallas_call | solution.py:205
  289.6 3.6 all-to-all-start.4
  295.1 5.4 %all-to-all-done.4 = bf16[4,592,128]{2,1,0:T(8,128)(2,1)S(1)} async-done(((bf16[4,592,128]{2,1,0:T(8,128)(2,1)}), bf16[4,592,128]{2,1,0:T(8,128)(2,1)S(1)}, u32[]{:S(2)}, u32[]{:S(2)}) %all-to-all-start.4) | async-done | bytes 606240 | tf_op jit(solution)/shard_map/all_to_all | solution.py:38
  303.7 3.7 all-to-all-start.5
  307.5 11.9 %all-to-all-done.5 = bf16[4,64,128]{2,1,0:T(8,128)(2,1)S(1)} async-done(((bf16[4,64,128]{2,1,0:T(8,128)(2,1)}), bf16[4,64,128]{2,1,0:T(8,128)(2,1)S(1)}, u32[]{:S(2)}, u32[]{:S(2)}) %all-to-all-start.5) | async-done | bytes 65568 | tf_op jit(solution)/shard_map/all_to_all | solution.py:38
  321.7 3.5 all-to-all-start.6
  325.4 6.7 %all-to-all-done.6 = bf16[4,512,128]{2,1,0:T(8,128)(2,1)S(1)} async-done(((bf16[4,512,128]{2,1,0:T(8,128)(2,1)}), bf16[4,512,128]{2,1,0:T(8,128)(2,1)S(1)}, u32[]{:S(2)}, u32[]{:S(2)}) %all-to-all-start.6) | async-done | bytes 524320 | tf_op jit(solution)/shard_map/all_to_all | solution.py:38
  332.9 11.2 %all-to-all-start.7 = ((bf16[8,112,128]{2,1,0:T(8,128)(2,1)}), bf16[8,112,128]{2,1,0:T(8,128)(2,1)S(1)}, u32[]{:S(2)}, u32[]{:S(2)}) async-start(bf16[8,112,128]{2,1,0:T(8,128)(2,1)} %maximum_maximum_fusion), calls=%async_computation.7 | async-start | bytes 458752 | tf_op jit(solution)/shard_map/all_to_all | solution.py:38
  344.2 6.2 %all-to-all-done.7 = bf16[8,112,128]{2,1,0:T(8,128)(2,1)S(1)} async-done(((bf16[8,112,128]{2,1,0:T(8,128)(2,1)}), bf16[8,112,128]{2,1,0:T(8,128)(2,1)S(1)}, u32[]{:S(2)}, u32[]{:S(2)}) %all-to-all-start.7) | async-done | bytes 229408 | tf_op jit(solution)/shard_map/all_to_all | solution.py:38
  350.8 15.2 %all_to_all.45 = bf16[16,16,128]{2,1,0:T(8,128)(2,1)S(1)} all-to-all(bf16[16,16,128]{2,1,0:T(8,128)(2,1)S(1)} %maximum_maximum_fusion.1), channel_id=1, replica_groups=mesh['zlo'=4,'x'=4,'core'=2,'y'=4,'zhi'=4] {'zlo','zhi'}, dimensions={0} | all-to-all | bytes 131072 | tf_op jit(solution)/shard_map/all_to_all | solution.py:38
  (175 shorter events, 43.7 us)
Async XLA Ops:
  7.2 34.7 %copy-start = (bf16[4096,64]{0,1:T(8,128)(2,1)S(1)}, bf16[4096,64]{0,1:T(8,128)(2,1)}, u32[]{:S(2)}) copy-start(bf16[4096,64]{0,1:T(8,128)(2,1)} %param.18) | copy-start | bytes 1572868
  11.7 11.2 %all-to-all-start.1 = ((bf16[4,384,128]{2,1,0:T(8,128)(2,1)}), bf16[4,384,128]{2,1,0:T(8,128)(2,1)S(1)}, u32[]{:S(2)}, u32[]{:S(2)}) async-start(bf16[4,384,128]{2,1,0:T(8,128)(2,1)} %broadcast_in_dim.37), calls=%async_computation.1 | async-start | bytes 786432 | tf_op jit(solution)/shard_map/all_to_all | solution.py:38
  23.7 41.5 %all-to-all-start = ((bf16[4,512,128]{2,1,0:T(8,128)(2,1)}), bf16[4,512,128]{2,1,0:T(8,128)(2,1)}, u32[]{:S(2)}, u32[]{:S(2)}) async-start(bf16[4,512,128]{2,1,0:T(8,128)(2,1)} %bitcast.3), calls=%async_computation | async-start | bytes 1048576 | tf_op jit(solution)/shard_map/all_to_all | solution.py:38
  39.1 2.7 copy-start.3
  40.2 2.1 copy-start.17
  40.2 2.1 copy-start.24
  42.6 29.0 %copy-start.25 = (s32[1,2048]{1,0:T(1,128)S(1)}, s32[1,2048]{1,0:T(1,128)}, u32[]{:S(2)}) copy-start(s32[1,2048]{1,0:T(1,128)} %param.17) | copy-start | bytes 24580
  65.2 34.3 %all-to-all-start.2 = ((bf16[4,1152,128]{2,1,0:T(8,128)(2,1)}), bf16[4,1152,128]{2,1,0:T(8,128)(2,1)}, u32[]{:S(2)}, u32[]{:S(2)}) async-start(bf16[4,1152,128]{2,1,0:T(8,128)(2,1)} %pad_maximum_fusion), calls=%async_computation.2 | async-start | bytes 2359296 | tf_op jit(solution)/shard_map/all_to_all | solution.py:38
  71.5 119.3 %all-gather.3.cloned.1.call-start = ((), (), s32[]{:S(2)}) async-start(), calls=%async_computation.9 | async-start | bytes 5652480 | tf_op jit(solution)/shard_map/all_gather | solution.py:307
  75.3 1.0 copy-start.9
  76.3 28.1 %copy-start.5 = (f32[512,128]{1,0:T(8,128)}, f32[512,128]{1,0:T(8,128)S(1)}, u32[]{:S(2)}) copy-start(f32[512,128]{1,0:T(8,128)S(1)} %get-tuple-element.92.sin_own_ref) | copy-start | bytes 786436
  100.6 1.6 copy-start.10
  102.1 1.2 copy-start.2
  106.0 2.0 copy-start.19
  213.6 41.1 %all-to-all-start.3 = ((bf16[4,512,128]{2,1,0:T(8,128)(2,1)}), bf16[4,512,128]{2,1,0:T(8,128)(2,1)}, u32[]{:S(2)}, u32[]{:S(2)}) async-start(bf16[4,512,128]{2,1,0:T(8,128)(2,1)} %broadcast_in_dim.39), calls=%async_computation.3 | async-start | bytes 1048576 | tf_op jit(solution)/shard_map/all_to_all | solution.py:38
  226.4 2.0 copy-start.12
  226.4 2.0 copy-start.14
  226.4 2.0 copy-start.16
  228.4 32.8 %copy-start.21 = (bf16[64,128]{1,0:T(8,128)(2,1)S(1)}, bf16[64,128]{1,0:T(8,128)(2,1)}, u32[]{:S(2)}) copy-start(bf16[64,128]{1,0:T(8,128)(2,1)} %slice_reduce_fusion.folded_ref) | copy-start | bytes 49156
  228.4 32.9 %copy-start.22 = (bf16[512,64]{1,0:T(8,128)(2,1)S(1)}, bf16[512,64]{1,0:T(8,128)(2,1)}, u32[]{:S(2)}) copy-start(bf16[512,64]{1,0:T(8,128)(2,1)} %get-tuple-element.19) | copy-start | bytes 196612
  257.7 5.3 %copy-start.7 = (bf16[512,128]{1,0:T(8,128)(2,1)}, bf16[512,128]{1,0:T(8,128)(2,1)S(1)}, u32[]{:S(2)}) copy-start(bf16[512,128]{1,0:T(8,128)(2,1)S(1)} %get-tuple-element.46.g_ref) | copy-start | bytes 393220
  282.0 2.4 copy-start.20
  282.0 4.3 %copy-start.23 = (bf16[4,64,128]{2,1,0:T(8,128)(2,1)S(1)}, bf16[4,64,128]{2,1,0:T(8,128)(2,1)}, u32[]{:S(2)}) copy-start(bf16[4,64,128]{2,1,0:T(8,128)(2,1)} %get-tuple-element.18) | copy-start | bytes 196612
  282.1 11.4 %copy-start.26 = (s32[32]{0:T(128)S(1)}, s32[32]{0:T(128)}, u32[]{:S(2)}) copy-start(s32[32]{0:T(128)} %param.28) | copy-start | bytes 388
  282.1 11.4 %copy-start.27 = (f32[32]{0:T(128)S(1)}, f32[32]{0:T(128)}, u32[]{:S(2)}) copy-start(f32[32]{0:T(128)} %param.27) | copy-start | bytes 388
  289.6 29.8 %copy-start.4 = (bf16[1,128,4096]{2,1,0:T(8,128)(2,1)S(1)}, bf16[1,128,4096]{2,1,0:T(8,128)(2,1)}, u32[]{:S(2)}) copy-start(bf16[1,128,4096]{2,1,0:T(8,128)(2,1)} %param.15) | copy-start | bytes 3145732
  289.6 11.0 %all-to-all-start.4 = ((bf16[4,592,128]{2,1,0:T(8,128)(2,1)}), bf16[4,592,128]{2,1,0:T(8,128)(2,1)S(1)}, u32[]{:S(2)}, u32[]{:S(2)}) async-start(bf16[4,592,128]{2,1,0:T(8,128)(2,1)} %constant_dynamic-update-slice_fusion.5), calls=%async_computation.4 | async-start | bytes 1212416 | tf_op jit(solution)/shard_map/all_to_all | solution.py:38
  303.7 15.6 %all-to-all-start.5 = ((bf16[4,64,128]{2,1,0:T(8,128)(2,1)}), bf16[4,64,128]{2,1,0:T(8,128)(2,1)S(1)}, u32[]{:S(2)}, u32[]{:S(2)}) async-start(bf16[4,64,128]{2,1,0:T(8,128)(2,1)} %pad_maximum_fusion.7), calls=%async_computation.5 | async-start | bytes 131072 | tf_op jit(solution)/shard_map/all_to_all | solution.py:38
  321.7 10.4 %all-to-all-start.6 = ((bf16[4,512,128]{2,1,0:T(8,128)(2,1)}), bf16[4,512,128]{2,1,0:T(8,128)(2,1)S(1)}, u32[]{:S(2)}, u32[]{:S(2)}) async-start(bf16[4,512,128]{2,1,0:T(8,128)(2,1)} %bitcast.60), calls=%async_computation.6 | async-start | bytes 1048576 | tf_op jit(solution)/shard_map/all_to_all | solution.py:38
  325.1 42.7 %copy-start.18 = (bf16[256,128]{1,0:T(8,128)(2,1)S(1)}, bf16[256,128]{1,0:T(8,128)(2,1)}, u32[]{:S(2)}) copy-start(bf16[256,128]{1,0:T(8,128)(2,1)} %param.22) | copy-start | bytes 196612
  325.1 43.5 %copy-start.1 = (bf16[4096,64]{0,1:T(8,128)(2,1)S(1)}, bf16[4096,64]{0,1:T(8,128)(2,1)}, u32[]{:S(2)}) copy-start(bf16[4096,64]{0,1:T(8,128)(2,1)} %param.18) | copy-start | bytes 1572868
  332.9 17.4 %all-to-all-start.7 = ((bf16[8,112,128]{2,1,0:T(8,128)(2,1)}), bf16[8,112,128]{2,1,0:T(8,128)(2,1)S(1)}, u32[]{:S(2)}, u32[]{:S(2)}) async-start(bf16[8,112,128]{2,1,0:T(8,128)(2,1)} %maximum_maximum_fusion), calls=%async_computation.7 | async-start | bytes 458752 | tf_op jit(solution)/shard_map/all_to_all | solution.py:38
  (5 other events, 4.3 us)
Sparse Core Ops, SparseCore 0:
  108.2 82.5 all-gather.2

commit v2 on v1

v2 whole, which is shorter than its diff:
```python
import math

import jax
import jax.numpy as jnp
from jax import lax
from jax.experimental import pallas as pl
from jax.experimental.pallas import tpu as pltpu
from jax.sharding import Mesh
from jax.sharding import PartitionSpec as P

STEPS = 10
ROPE_BASE = 10000.0
ETA = 0.7
CLIP = 0.05
ADV_FLOOR = 0.5

NAMES = ("zlo", "x", "core", "y", "zhi")
SIZES = (4, 4, 2, 4, 4)
DP = ("zlo", "x", "core")
SEQ = ("y", "zhi")
XC = ("x", "core")
Z = ("zlo", "zhi")

HEADS = 4
TOK = 128
OWN = 512
LENGTH = 2048
HD = 128
RANK = 64
SCALE = 1.0 / math.sqrt(HD)
F32 = jnp.float32
BF16 = jnp.bfloat16
VMEM_LIMIT = 56 * 1024 * 1024


def exchange(pieces, axes):
    return lax.all_to_all(pieces, axes, split_axis=0, concat_axis=0, tiled=True)


def dot(a, b, dims=(1, 0)):
    return lax.dot_general(a, b, (((dims[0],), (dims[1],)), ((), ())), preferred_element_type=F32)


def gap_factor(denoising_step_index):
    noise_level = 1.0 - denoising_step_index[0].astype(F32) / STEPS
    step_width = 1.0 / STEPS
    sigma_value = ETA * jnp.sqrt(noise_level / (1.0 - noise_level))
    spread_value = sigma_value * math.sqrt(step_width)
    drift_coef = sigma_value * sigma_value / (2.0 * noise_level)
    return step_width * (1.0 + drift_coef * (1.0 - noise_level)) / spread_value


def advantages(rewards, rollout_group_index):
    same_group = (rollout_group_index[:, None] == rollout_group_index[None, :]).astype(F32)
    group_size = jnp.sum(same_group, axis=1)
    group_mean = jnp.sum(same_group * rewards[None, :], axis=1) / group_size
    centred = rewards[None, :] - group_mean[:, None]
    group_var = jnp.sum(same_group * centred * centred, axis=1) / group_size
    return (rewards - group_mean) / jnp.maximum(jnp.sqrt(group_var), ADV_FLOOR)


def rope_tables(frame_row):
    half = HD // 2
    inverse = ROPE_BASE ** (-jnp.arange(half, dtype=F32) / half)
    angles = frame_row.astype(F32)[:, None] * inverse[None, :]
    cos, sin = jnp.cos(angles), jnp.sin(angles)
    return jnp.concatenate([cos, cos], axis=1), jnp.concatenate([-sin, sin], axis=1)


def call(kernel, name, grid, in_specs, out_specs, out_shape, scratch=(), prefetch=0):
    return pl.pallas_call(
        kernel,
        grid_spec=pltpu.PrefetchScalarGridSpec(
            num_scalar_prefetch=prefetch,
            grid=grid,
            in_specs=in_specs,
            out_specs=out_specs,
            scratch_shapes=list(scratch),
        ),
        out_shape=out_shape,
        compiler_params=pltpu.CompilerParams(vmem_limit_bytes=VMEM_LIMIT),
        name=name,
    )


def whole(*dims):
    return pl.BlockSpec(dims, lambda *_: (0,) * len(dims))


def per_head(*dims):
    return pl.BlockSpec((1,) + dims, lambda h, *_: (h,) + (0,) * len(dims))


def pick(dims, index):
    return pl.BlockSpec(dims, lambda h, *_: index(h))


def shape(dims, kind=BF16):
    return jax.ShapeDtypeStruct(dims, kind)


KV_ROWS = 8 * TOK + RANK
Q_ROWS = 4 * TOK + RANK
IN_ROWS = 512
HEAD_ROWS = 5 * RANK + 16


def pack_kernel(frozen_ref, normed_ref, down_ref, kv_ref, q_ref):
    out = lax.broadcasted_iota(jnp.int32, (256, 256), 0)
    source = lax.broadcasted_iota(jnp.int32, (256, 256), 1)
    order = (source == (out % 16) * 16 + ((out // 16) % 4) * 4 + out // 64).astype(BF16)
    for group in range(TOK // 16):
        rows = dot(order, frozen_ref[pl.ds(group * 256, 256), :]).astype(BF16)
        for zhi in range(4):
            for y in range(4):
                part = rows[(zhi * 4 + y) * 16 : (zhi * 4 + y) * 16 + 16]
                here = y * TOK + group * 16
                q_ref[zhi, pl.ds(here, 16), :] = part[:, :HD]
                kv_ref[zhi, pl.ds(here, 16), :] = part[:, HD : 2 * HD]
                kv_ref[zhi, pl.ds(4 * TOK + here, 16), :] = part[:, 2 * HD :]
    down_rows = dot(normed_ref[...], down_ref[...]).T.astype(BF16)
    for zhi in range(4):
        kv_ref[zhi, pl.ds(8 * TOK, RANK), :] = down_rows


def pack(frozen, normed, qkv_down):
    return call(
        pack_kernel,
        "pack",
        (1,),
        [whole(TOK * 16, 3 * HD), whole(TOK, 4096), whole(4096, RANK)],
        [whole(4, KV_ROWS, HD), whole(4, 4 * TOK, HD)],
        [shape((4, KV_ROWS, HD)), shape((4, 4 * TOK, HD))],
    )(frozen, normed, qkv_down)


def adapters_kernel(up_ref, ad_ref, rh_ref, out_up_ref, readout_ref, pack_ref):
    for part in range(3):
        pack_ref[pl.ds(part * RANK, RANK), :] = up_ref[:, part * HD : part * HD + HD]
    pack_ref[pl.ds(3 * RANK, RANK), :] = ad_ref[...].astype(F32).T.astype(BF16)
    pack_ref[pl.ds(4 * RANK, HD), :] = rh_ref[...]
    pack_ref[pl.ds(4 * RANK + HD, RANK), :] = dot(out_up_ref[...], readout_ref[...]).astype(BF16)


def adapters(up, ad, rh, out_up, readout):
    rows = 5 * RANK + HD
    return call(
        adapters_kernel,
        "adapters",
        (1,),
        [whole(RANK, 3 * HD), whole(HD, RANK), whole(HD, HD), whole(RANK, 256), whole(256, HD)],
        whole(rows, HD),
        shape((rows, HD)),
    )(up, ad, rh, out_up, readout)


def forward_kernel(*refs):
    keys, values, downs = refs[0:5], refs[5:10], refs[10:15]
    q_ref, fold_ref, wt_ref, cos_ref, sin_ref = refs[15:20]
    (att_ref, prob_ref, inv_ref, qo_ref, ko_ref, vo_ref, vel_ref, od_ref, folded_ref, dt_ref) = refs[20:30]
    rows_ref, vel_acc, od_acc = refs[30:]
    head = pl.program_id(0)

    def blocks(group):
        return [ref[i] for ref in group for i in range(ref.shape[0])]

    @pl.when(head == 0)
    def _():
        folded = fold_ref[0].astype(F32)
        for i in range(1, 4):
            folded = folded + fold_ref[i].astype(F32)
        folded_ref[...] = folded.astype(BF16)
        for i, block in enumerate(blocks(downs)):
            dt_ref[:, i * TOK : i * TOK + TOK] = block
            rows_ref[pl.ds(i * TOK, TOK), :] = block.astype(F32).T.astype(BF16)

    def rotated(tensor, cos, sin):
        return (tensor * cos + pltpu.roll(tensor, HD // 2, 1) * sin).astype(BF16)

    wt = wt_ref[0]
    down_rows = rows_ref[...]
    raw = jnp.concatenate([q_ref[i] for i in range(4)], axis=0).astype(F32)
    q = rotated(raw + dot(down_rows[:OWN], wt[:RANK]), cos_ref[:OWN, :], sin_ref[:OWN, :])
    raw = jnp.concatenate(blocks(keys), axis=0).astype(F32)
    k = rotated(raw + dot(down_rows, wt[RANK : 2 * RANK]), cos_ref[...], sin_ref[...])
    raw = jnp.concatenate(blocks(values), axis=0).astype(F32)
    v = (raw + dot(down_rows, wt[2 * RANK : 3 * RANK])).astype(BF16)
    qo_ref[0] = q
    ko_ref[0] = k
    vo_ref[0] = v
    scores = dot(k, q, (1, 1))
    peak = jnp.max(scores, axis=0, keepdims=True)
    weights = jnp.exp((scores - peak) * SCALE)
    inverse = 1.0 / jnp.sum(weights, axis=0, keepdims=True)
    weights = weights.astype(BF16)
    prob_ref[0] = weights
    inv_ref[0] = inverse
    attended = dot(v, weights, (0, 0)) * inverse
    att = attended.T.astype(BF16)
    att_ref[0] = att
    velocity = dot(att, wt[4 * RANK : 4 * RANK + HD])
    down = dot(att, wt[3 * RANK : 4 * RANK], (1, 1))

    @pl.when(head == 0)
    def _():
        vel_acc[...] = velocity
        od_acc[...] = down

    @pl.when(head > 0)
    def _():
        vel_acc[...] += velocity
        od_acc[...] += down

    @pl.when(head == HEADS - 1)
    def _():
        out_down = od_acc[...].astype(BF16)
        od_ref[...] = out_down
        vel_ref[...] = (vel_acc[...] + dot(out_down, folded_ref[...])).astype(BF16)


def forward(gathered, q, wts, cos, sin):
    def each(rows, index):
        return [pick((block.shape[0], rows, HD), index) for block in gathered]

    return call(
        forward_kernel,
        "attention_forward",
        (HEADS,),
        each(TOK, lambda h: (0, h, 0))
        + each(TOK, lambda h: (0, 4 + h, 0))
        + each(RANK, lambda h: (0, 8 * TOK // RANK, 0))
        + [
            pick((4, TOK, HD), lambda h: (0, h, 0)),
            pick((4, RANK, HD), lambda h: (0, 4 * TOK // RANK, 0)),
            per_head(5 * RANK + HD, HD),
            whole(LENGTH, HD),
            whole(LENGTH, HD),
        ],
        [
            per_head(OWN, HD),
            per_head(LENGTH, OWN),
            per_head(1, OWN),
            per_head(OWN, HD),
            per_head(LENGTH, HD),
            per_head(LENGTH, HD),
            whole(OWN, HD),
            whole(OWN, RANK),
            whole(RANK, HD),
            whole(RANK, LENGTH),
        ],
        [
            shape((HEADS, OWN, HD)),
            shape((HEADS, LENGTH, OWN)),
            shape((HEADS, 1, OWN), F32),
            shape((HEADS, OWN, HD)),
            shape((HEADS, LENGTH, HD)),
            shape((HEADS, LENGTH, HD)),
            shape((OWN, HD)),
            shape((OWN, RANK)),
            shape((RANK, HD)),
            shape((RANK, LENGTH)),
        ],
        [pltpu.VMEM((LENGTH, RANK), BF16), pltpu.VMEM((OWN, HD), F32), pltpu.VMEM((OWN, RANK), F32)],
    )(*gathered, *gathered, *gathered, q, q, wts, cos, sin)


def unrotate(grad, cos, sin):
    return (grad * cos - pltpu.roll(grad, HD // 2, 1) * sin).astype(BF16)


def backward_kernel(
    y_ref, mult_ref, vel_ref, res_ref, samp_ref, noise_ref, folded_ref, od_ref, q_ref, k_ref, v_ref, prob_ref,
    inv_ref, att_ref, wt_ref, dt_ref, cos_ref, sin_ref, dgrad_ref, small_ref, g_ref, og_ref, fg_ref, log_ref, dg_acc,
):
    head = pl.program_id(0)

    @pl.when(head == 0)
    def _():
        velocity = vel_ref[0].astype(F32)
        for i in range(1, 4):
            velocity = velocity + vel_ref[i].astype(F32)
        velocity = res_ref[0].astype(F32) + velocity
        gap = mult_ref[0, 0] * (velocity - samp_ref[0].astype(F32))
        noise = noise_ref[0].astype(F32)
        terms = jnp.sum(noise * gap + 0.5 * gap * gap, axis=0, keepdims=True)
        log = jnp.sum(terms, axis=1, keepdims=True) * (-1.0 / (LENGTH * HD))
        high = log.astype(BF16).astype(F32)
        middle = (log - high).astype(BF16).astype(F32)
        low = log - high - middle
        lane = lax.broadcasted_iota(jnp.int32, (16, HD), 1)
        rows = jnp.where(lane == 0, high, jnp.where(lane == 1, middle, jnp.where(lane == 2, low, 0.0)))
        log_ref[...] = rows.astype(BF16)
        g = (noise + gap).astype(BF16)
        g_ref[...] = g
        og_ref[...] = dot(g, folded_ref[...], (1, 1)).astype(BF16)
        fg_ref[...] = dot(od_ref[...], g, (0, 0)).astype(BF16)

    wt = wt_ref[0]
    att = att_ref[0]
    og = og_ref[...]
    att_grad = dot(g_ref[...], wt[4 * RANK : 4 * RANK + HD], (1, 1)) + dot(og, wt[3 * RANK : 4 * RANK])
    att_grad = att_grad.astype(BF16).astype(F32)
    inverse = inv_ref[0]
    delta = jnp.sum((att_grad * att.astype(F32)).T, axis=0, keepdims=True) * inverse
    scaled = (att_grad * jnp.broadcast_to(inverse, (HD, OWN)).T).astype(BF16)
    weights = prob_ref[0]
    prob_grad = dot(v_ref[0], scaled, (1, 1))
    score_grad = (weights.astype(F32) * (prob_grad - delta)).astype(BF16)
    v_grad = dot(weights, scaled).astype(BF16)
    k_grad = unrotate(dot(score_grad, q_ref[0]) * SCALE, cos_ref[...], sin_ref[...])
    q_grad = dot(k_ref[0], score_grad, (0, 0)) * SCALE
    q_grad = unrotate(q_grad.T, cos_ref[:OWN, :], sin_ref[:OWN, :])
    share = dot(wt[RANK : 2 * RANK], k_grad, (1, 1)) + dot(wt[2 * RANK : 3 * RANK], v_grad, (1, 1))
    mine = share[:, :OWN] + dot(wt[:RANK], q_grad, (1, 1))

    @pl.when(head == 0)
    def _():
        dg_acc[:, :OWN] = mine
        dg_acc[:, OWN:] = share[:, OWN:]

    @pl.when(head > 0)
    def _():
        dg_acc[:, :OWN] += mine
        dg_acc[:, OWN:] += share[:, OWN:]

    down_t = dt_ref[...]
    small_ref[0, :RANK, :] = dot(down_t[:, :OWN], q_grad).astype(BF16)
    small_ref[0, RANK : 2 * RANK, :] = dot(down_t, k_grad).astype(BF16)
    small_ref[0, 2 * RANK : 3 * RANK, :] = dot(down_t, v_grad).astype(BF16)
    small_ref[0, 3 * RANK : 4 * RANK, :] = dot(og, att, (0, 0)).astype(BF16)
    small_ref[0, 4 * RANK : 5 * RANK, :] = fg_ref[...]
    small_ref[0, 5 * RANK :, :] = log_ref[...]

    @pl.when(head == HEADS - 1)
    def _():
        for near in range(4):
            for zhi in range(4):
                place = ((y_ref[0] + near) % 4) * 4 + zhi
                first = (near * 4 + zhi) * TOK
                dgrad_ref[pl.ds(place, 1)] = dg_acc[:, first : first + TOK].astype(BF16)[None]


def backward(y, mult, velocity, residual, sampling, noise, folded, out_down, q, k, v, prob, inv, att, wts, down_t, cos, sin):
    mine = pl.BlockSpec((1, OWN, HD), lambda h, y_ref: (0, y_ref[0], 0))
    return call(
        backward_kernel,
        "attention_backward",
        (HEADS,),
        [
            pl.BlockSpec(memory_space=pltpu.SMEM),
            whole(4, OWN, HD),
            mine,
            mine,
            mine,
            whole(RANK, HD),
            whole(OWN, RANK),
            per_head(OWN, HD),
            per_head(LENGTH, HD),
            per_head(LENGTH, HD),
            per_head(LENGTH, OWN),
            per_head(1, OWN),
            per_head(OWN, HD),
            per_head(5 * RANK + HD, HD),
            whole(RANK, LENGTH),
            whole(LENGTH, HD),
            whole(LENGTH, HD),
        ],
        [whole(16, RANK, TOK), per_head(HEAD_ROWS, HD)],
        [shape((16, RANK, TOK)), shape((HEADS, HEAD_ROWS, HD))],
        [
            pltpu.VMEM((OWN, HD), BF16),
            pltpu.VMEM((OWN, RANK), BF16),
            pltpu.VMEM((RANK, HD), BF16),
            pltpu.VMEM((16, HD), BF16),
            pltpu.VMEM((RANK, LENGTH), F32),
        ],
        prefetch=1,
    )(y, mult, velocity, residual, sampling, noise, folded, out_down, q, k, v, prob, inv, att, wts, down_t, cos, sin)


def grad_in_kernel(shares_ref, normed_ref, small_ref, out_ref):
    down_grad = shares_ref[0].astype(F32)
    for i in range(1, 16):
        down_grad = down_grad + shares_ref[i].astype(F32)
    grad = dot(down_grad.astype(BF16), normed_ref[...])
    for j in range(16):
        left = grad[:, j * TOK : j * TOK + TOK]
        right = grad[:, 2048 + j * TOK : 2048 + j * TOK + TOK]
        block = jnp.concatenate([left, right], axis=0).T.astype(BF16)
        for y in range(4):
            out_ref[y, pl.ds(j * 32, 32), :] = block[y * 32 : y * 32 + 32]
    for y in range(4):
        out_ref[y, pl.ds(IN_ROWS, HEAD_ROWS), :] = small_ref[y]


def grad_in_part(shares, normed, small):
    rows = IN_ROWS + HEAD_ROWS
    return call(
        grad_in_kernel,
        "grad_in_part",
        (1,),
        [whole(16, RANK, TOK), whole(TOK, 4096), whole(4, HEAD_ROWS, HD)],
        whole(4, rows, HD),
        shape((4, rows, HD)),
    )(shares, normed, small)


def weigh_kernel(scal_ref, got_ref, out_ref):
    total = got_ref[0].astype(F32)
    for i in range(1, 4):
        total = total + got_ref[i].astype(F32)
    lane = lax.broadcasted_iota(jnp.int32, (8, HD), 1)
    log = total[IN_ROWS + 5 * RANK : IN_ROWS + 5 * RANK + 8]
    log = jnp.sum(jnp.where(lane < 3, log, 0.0), axis=1, keepdims=True)
    ratio = jnp.exp(log[:1])
    advantage = scal_ref[0, 0]
    positive = jnp.where(advantage >= 0.0, 1.0, 0.0)
    active = jnp.where(ratio <= 1.0 + CLIP, positive, 0.0) + jnp.where(ratio >= 1.0 - CLIP, 1.0 - positive, 0.0)
    weight = jnp.where(active > 0.5, -advantage * scal_ref[0, 1] * ratio, 0.0)
    total = total[: IN_ROWS + 5 * RANK] * weight
    for xc in range(8):
        for low in range(2):
            out_ref[xc, pl.ds(low * 32, 32), :] = total[(low * 8 + xc) * 32 : (low * 8 + xc) * 32 + 32].astype(BF16)
    out = lax.broadcasted_iota(jnp.int32, (RANK, RANK), 0)
    source = lax.broadcasted_iota(jnp.int32, (RANK, RANK), 1)
    order = (source == ((out // 2) % 4) * 16 + (out // 8) * 2 + out % 2).astype(BF16)
    parts = []
    for i in range(5):
        rows = total[IN_ROWS + i * RANK : IN_ROWS + i * RANK + RANK].astype(BF16)
        parts.append(dot(order, rows))
    for xc in range(8):
        rows = [part[xc * 8 : xc * 8 + 8] for part in parts] + [jnp.zeros((8, HD), F32)]
        out_ref[xc, pl.ds(64, 48), :] = jnp.concatenate(rows, axis=0).astype(BF16)


def weigh(scalars, got):
    return call(
        weigh_kernel,
        "weigh",
        (1,),
        [pl.BlockSpec(memory_space=pltpu.SMEM), whole(4, IN_ROWS + HEAD_ROWS, HD)],
        whole(8, 112, HD),
        shape((8, 112, HD)),
    )(scalars, got)


def body(
    normed,
    frozen,
    frames,
    qkv_down,
    qkv_up,
    out_down_adapter,
    out_up,
    readout,
    readout_head,
    residual_velocity,
    sampling_velocity,
    sampler_step_noise,
    rewards,
    rollout_group_index,
    denoising_step_index,
):
    y = lax.axis_index("y")
    zhi = lax.axis_index("zhi")
    ahead = [(i, (i + 1) % 4) for i in range(4)]
    back = [(i, (i + 3) % 4) for i in range(4)]

    send_kv, send_q = pack(frozen.reshape(TOK * 16, 3 * HD), normed[0], qkv_down)
    mine = exchange(send_kv, "zhi")
    before = lax.ppermute(mine, "y", ahead)
    after = lax.ppermute(mine, "y", back)
    far_low = lax.ppermute(after[:2], "y", back)
    far_high = lax.ppermute(before[2:], "y", ahead)

    wts = adapters(qkv_up[:, 0], out_down_adapter[0], readout_head[0], out_up, readout)
    wts = lax.all_gather(wts, "y", axis=0, tiled=False)
    fold_y = jnp.sum(wts[:, 4 * RANK + HD :].astype(F32), axis=0).astype(BF16)
    fold_y = jnp.broadcast_to(fold_y[None], (4, RANK, HD))
    q_raw = exchange(jnp.concatenate([send_q, fold_y], axis=1), "zhi")

    multiplier = gap_factor(denoising_step_index)
    advantage = advantages(rewards, rollout_group_index)[lax.axis_index(DP)]
    scalars = jnp.stack([advantage, multiplier])[None]
    cos, sin = rope_tables(jnp.roll(frames[0], -y * OWN))

    att, prob, inv, q, k, v, vel_part, out_down, folded, down_t = forward(
        (mine, after, far_low, far_high, before), q_raw, wts, cos, sin
    )
    velocity = lax.all_gather(vel_part, "zhi", axis=0, tiled=False)
    down_grad, small = backward(
        y[None].astype(jnp.int32), multiplier[None, None], velocity, residual_velocity, sampling_velocity,
        sampler_step_noise, folded, out_down, q, k, v, prob, inv, att, wts, down_t, cos, sin,
    )

    down_grad = exchange(down_grad, SEQ)
    both = weigh(scalars, exchange(grad_in_part(down_grad, normed[0], small), "y"))
    both = jnp.sum(exchange(both, XC).astype(F32), axis=0)
    in_part = both[:64].reshape(2, 4, 8, 2, 64).transpose(3, 0, 1, 2, 4).reshape(4, 4, 4, HD)
    small = both[64:104].reshape(5, 4, 2, HD).transpose(1, 2, 0, 3).reshape(4, 1, 10, HD)
    here = (lax.broadcasted_iota(jnp.int32, (4, 4, 10, HD), 1) == zhi).astype(F32)
    everywhere = lax.broadcasted_iota(jnp.int32, (4, 4, 10, HD), 2) % 5 == 4
    small = small * jnp.where(everywhere, 1.0, here)
    last = jnp.concatenate([in_part, small, jnp.zeros((4, 4, 2, HD), F32)], axis=2).astype(BF16)
    last = jnp.sum(exchange(last.reshape(16, 16, HD), Z).astype(F32), axis=0)
    grad_in = last[:4].reshape(8, 64)
    small = last[4:14].reshape(2, 5, HD)
    grad_qkv = small[:, None, :3].reshape(2, 1, 3 * HD)
    grad_out_in = small[:, 3].T[None]
    grad_out = lax.dot_general(
        small[:, 4], readout.astype(F32), (((1,), (1,)), ((), ())), precision=lax.Precision.HIGHEST
    )
    return grad_in, grad_qkv, grad_out_in, grad_out


def solution(mesh):
    mesh = Mesh(mesh.devices.reshape(SIZES), NAMES)
    in_specs = (
        P(DP, SEQ, None),
        P(DP, SEQ, None, None),
        P(DP, None),
        P(),
        P(None, SEQ, None),
        P(SEQ, None, None),
        P(None, SEQ),
        P(SEQ, None),
        P(SEQ, None, None),
        P(DP, None, None),
        P(DP, None, None),
        P(DP, None, None),
        P(),
        P(),
        P(),
    )
    out_specs = (P(DP + SEQ, None), P(DP, SEQ, None), P(SEQ, None, DP), P(DP, SEQ))
    return jax.shard_map(body, mesh=mesh, in_specs=in_specs, out_specs=out_specs, check_vma=False)
```

time: 377 us -> 271 us (0.72)
  waiting for transfers between devices: 179 us -> 79.7 us
  blocking collectives: 15.2 us -> 62.1 us
  local copies, waits for them, and re-layouts: 38.4 us -> 9.3 us
  between operations: 21.1 us -> 1.74 us
  other arithmetic: 25.4 us -> 10.4 us
  Pallas kernels: 33.1 us -> 46.3 us
    all_gather x1 -> x0, waiting for transfers between devices: 80.4 us -> none  [body(): shared = lax.all_gather(shared, 'y', axis=0, tiled=False)]
    all_gather x0 -> x2, blocking collectives: none -> 41.3 us  [the longest x1 28.4 us: body(): velocity = lax.all_gather(vel_part, 'zhi', axis=0, tiled=False)]
    all_to_all x8 -> x5, waiting for transfers between devices: 98.4 us -> 65.2 us  [exchange(): return lax.all_to_all(pieces, axes, split_axis=0, concat_axis=0, tiled=True)]
    all_to_all x8 -> x5, starting transfers between devices: 60.7 us -> 45.3 us  [exchange(): return lax.all_to_all(pieces, axes, split_axis=0, concat_axis=0, tiled=True)]
    ppermute x0 -> x4, waiting for transfers between devices: none -> 14.4 us  [the longest x1 8.86 us: body(): after = lax.ppermute(mine, 'y', back)]
    ppermute x0 -> x4, starting transfers between devices: none -> 13.9 us  [the longest x1 5.41 us: body(): far_low = lax.ppermute(after[:2], 'y', back)]
    pallas_call x2 -> x6, Pallas kernels: 33.1 us -> 46.3 us  [the longest x1 18.3 us: backward(): call(backward_kernel, 'attention_backward', (HEADS,), [pl.BlockSpec(memor...]
    slice x16 -> x3, local copies, waits for them, and re-layouts: 13.3 us -> 0.93 us  [the longest x1 0.88 us: body(): far_low = lax.ppermute(after[:2], 'y', back)]
  transfers between devices with their start and end apart: 9 -> 9, of which waited for: 9 -> 7; matrix products, arithmetic and copies ran while one was open for 6% -> 5% of each run, Pallas kernels for 0% -> 1%
where the time goes in v2:
time: 271 us; the launch traced here: 269 us
  waiting for transfers between devices  79.7 us (29%)
  blocking collectives  62.1 us (23%)
  starting transfers between devices  59.2 us (22%)
  Pallas kernels  46.3 us (17%)
  other arithmetic  10.4 us (4%)
  local copies, waits for them, and re-layouts  9.3 us (3%)
    all_to_all x5, waiting for transfers between devices, exchange(): return lax.all_to_all(pieces, axes, split_axis=0, concat_axis=0, tiled=True)  65.2 us
    all_to_all x5, starting transfers between devices, exchange(): return lax.all_to_all(pieces, axes, split_axis=0, concat_axis=0, tiled=True)  45.3 us
    all_gather x1, blocking collectives, body(): velocity = lax.all_gather(vel_part, 'zhi', axis=0, tiled=False)  28.4 us
    all_to_all x1, blocking collectives, exchange(): return lax.all_to_all(pieces, axes, split_axis=0, concat_axis=0, tiled=True)  20.8 us
    pallas_call x1, Pallas kernels, backward(): call(backward_kernel, 'attention_backward', (HEADS,), [pl.BlockSpec(memor...  18.3 us
    pallas_call x1, Pallas kernels, forward(): call(forward_kernel, 'attention_forward', (HEADS,), each(TOK, lambda h: (...  17.5 us
    all_gather x1, blocking collectives, body(): wts = lax.all_gather(wts, 'y', axis=0, tiled=False)  12.9 us
    ppermute x1, waiting for transfers between devices, body(): after = lax.ppermute(mine, 'y', back)  8.86 us
  transfers between devices with their start and end apart: 9, of which 7 were waited for; matrix products, arithmetic and copies ran while one was open for 5% of the time, Pallas kernels for 1%

profile of v2, /device:TPU:1, one launch (start us, length us, event | category | flops | bytes accessed | tf_op | source)
XLA Modules:
  0.0 269.5 jit_solution(8248806796996844529)
XLA Ops:
  0.6 2.4 copy.31.down_ref
  3.0 4.0 %pack.1 = (bf16[4,1088,128]{2,1,0:T(8,128)(2,1)}, bf16[4,512,128]{2,1,0:T(8,128)(2,1)}) custom-call(bf16[2048,384]{1,0:T(8,128)(2,1)} %bitcast.39, bf16[128,4096]{1,0:T(8,128)(2,1)} %bitcast.36, bf16[4096,64]{1,0:T(8,128)(2,1)} %copy.31.down_ref), custom_call_target="tpu_custom_call" | custom-call | tf_op jit(solution)/shard_map/pack/pallas_call | solution.py:127
  7.1 15.8 %all-to-all-start = ((bf16[4,1088,128]{2,1,0:T(8,128)(2,1)}), bf16[4,1088,128]{2,1,0:T(8,128)(2,1)S(1)}, u32[]{:S(2)}, u32[]{:S(2)}) async-start(bf16[4,1088,128]{2,1,0:T(8,128)(2,1)} %get-tuple-element.18), calls=%async_computation | async-start | bytes 2228224 | tf_op jit(solution)/shard_map/all_to_all | solution.py:37
  23.5 1.7 adapters.1
  25.3 12.9 %all-gather = bf16[1792,128]{1,0:T(8,128)(2,1)} all-gather(bf16[448,128]{1,0:T(8,128)(2,1)} %adapters.1), channel_id=2, replica_groups=mesh['zlo'=4,'x'=4,'core'=2,'y'=4,'zhi'=4] {'y'}, dimensions={0}, use_global_device_ids=true | all-gather | bytes 573440 | tf_op jit(solution)/shard_map/all_gather | solution.py:477
  38.1 37.2 %all-to-all-done.refs_0_.refs_5_.refs_10_ = bf16[4,1088,128]{2,1,0:T(8,128)(2,1)S(1)} async-done(((bf16[4,1088,128]{2,1,0:T(8,128)(2,1)}), bf16[4,1088,128]{2,1,0:T(8,128)(2,1)S(1)}, u32[]{:S(2)}, u32[]{:S(2)}) %all-to-all-start) | async-done | bytes 1114144 | tf_op jit(solution)/shard_map/all_to_all | solution.py:37
  75.4 4.6 %collective-permute-start = (bf16[4,1088,128]{2,1,0:T(8,128)(2,1)S(1)}, bf16[4,1088,128]{2,1,0:T(8,128)(2,1)S(1)}, u32[]{:S(2)}, u32[]{:S(2)}) collective-permute-start(bf16[4,1088,128]{2,1,0:T(8,128)(2,1)S(1)} %all-to-all-done.refs_0_.refs_5_.refs_10_), channel_id=1, source_target_pairs={{0,12},{4,0},{8,4},{12,8},{1,13},{5,1},{9,5},{13,9},{2,14},{6,2},{... | collective-permute-start | bytes 3342344 | tf_op jit(solution)/shard_map/ppermute | solution.py:472
  80.0 1.9 collective-permute-start.2
  82.0 0.9 slice_reduce_fusion
  82.8 1.9 pad_maximum_fusion.2
  84.8 6.4 %all-to-all-start.1 = ((bf16[4,576,128]{2,1,0:T(8,128)(2,1)}), bf16[4,576,128]{2,1,0:T(8,128)(2,1)}, u32[]{:S(2)}, u32[]{:S(2)}) async-start(bf16[4,576,128]{2,1,0:T(8,128)(2,1)} %pad_maximum_fusion.2), calls=%async_computation.1 | async-start | bytes 1179648 | tf_op jit(solution)/shard_map/all_to_all | solution.py:37
  92.1 8.9 %collective-permute-done.refs_1_.refs_6_.refs_11_ = bf16[4,1088,128]{2,1,0:T(8,128)(2,1)S(1)} collective-permute-done((bf16[4,1088,128]{2,1,0:T(8,128)(2,1)S(1)}, bf16[4,1088,128]{2,1,0:T(8,128)(2,1)S(1)}, u32[]{:S(2)}, u32[]{:S(2)}) %collective-permute-start) | collective-permute-done | bytes 1114144 | tf_op jit(solution)/shard_map/ppermute | solution.py:472
  101.0 0.9 slice.41
  101.8 5.4 %collective-permute-start.1 = (bf16[2,1088,128]{2,1,0:T(8,128)(2,1)}, bf16[2,1088,128]{2,1,0:T(8,128)(2,1)}, u32[]{:S(2)}, u32[]{:S(2)}) collective-permute-start(bf16[2,1088,128]{2,1,0:T(8,128)(2,1)} %slice.41), channel_id=1, source_target_pairs={{0,12},{4,0},{8,4},{12,8},{1,13},{5,1},{9,5},{13,9},{2,14},{6,2},{... | collective-permute-start | bytes 1671176 | tf_op jit(solution)/shard_map/ppermute | solution.py:473
  107.3 1.9 collective-permute-start.3
  109.3 3.7 %fusion = (f32[2048,64]{1,0:T(8,128)S(1)}, f32[2048,64]{1,0:T(8,128)S(1)}, f32[2048,64]{1,0:T(8,128)S(1)}) fusion(f32[64]{0:T(128)S(1)} %multiply_power_fusion, f32[2048]{0:T(1024)S(1)} %fusion.7), kind=kLoop, calls=%fused_computation.6 | loop fusion | flops 262144 | bytes 1581312 | tf_op jit(solution)/shard_map/neg | solution.py:67
  113.0 1.9 pad_maximum_fusion
  115.7 4.8 %collective-permute-done.3.refs_3_.refs_8_.refs_13_ = bf16[2,1088,128]{2,1,0:T(8,128)(2,1)S(1)} collective-permute-done((bf16[2,1088,128]{2,1,0:T(8,128)(2,1)S(1)}, bf16[2,1088,128]{2,1,0:T(8,128)(2,1)S(1)}, u32[]{:S(2)}, u32[]{:S(2)}) %collective-permute-start.3) | collective-permute-done | bytes 557088 | tf_op jit(solution)/shard_map/ppermute | solution.py:474
  121.4 17.5 %attention_forward.1 = (bf16[4,512,128]{2,1,0:T(8,128)(2,1)}, bf16[4,2048,512]{2,1,0:T(8,128)(2,1)}, f32[4,1,512]{2,1,0:T(1,128)}, bf16[4,512,128]{2,1,0:T(8,128...) custom-call(bf16[4,1088,128]{2,1,0:T(8,128)(2,1)} %copy-done, ...), custom_call_target="tpu_custom_call" | custom-call | tf_op jit(solution)/shard_map/attention_forward/pallas_call | solution.py:225
  138.8 28.4 %all-gather.1 = bf16[2048,128]{1,0:T(8,128)(2,1)} all-gather(bf16[512,128]{1,0:T(8,128)(2,1)} %get-tuple-element.20), channel_id=3, replica_groups=mesh['zlo'=4,'x'=4,'core'=2,'y'=4,'zhi'=4] {'zhi'}, dimensions={0}, use_global_device_ids=true | all-gather | bytes 655360 | tf_op jit(solution)/shard_map/all_gather | solution.py:490
  167.2 18.3 %attention_backward.1 = (bf16[16,64,128]{2,1,0:T(8,128)(2,1)}, bf16[4,336,128]{2,1,0:T(8,128)(2,1)}) custom-call(s32[1]{0:T(128)} %bitcast.3.y_ref, f32[1,1]{1,0:T(1,128)} %bitcast.4.mult_ref, bf16[4,512,128]{2,1,0:T(8,128)(2,1)} %bitcast.38, bf16[1,2048,128]{2,1,0:T(8,128)(2,1)} %res_ref.1, bf16[1,2048,128]{2,1,0:T(8,128)(2,1)} %samp_ref.1, ...), custom_call_target="tpu_custom_call" | custom-call | tf_op jit(solution)/shard_map/attention_backward/pallas_call | solution.py:345
  185.5 6.5 %all-to-all-start.2 = ((bf16[16,64,128]{2,1,0:T(8,128)(2,1)}), bf16[16,64,128]{2,1,0:T(8,128)(2,1)S(1)}, u32[]{:S(2)}, u32[]{:S(2)}) async-start(bf16[16,64,128]{2,1,0:T(8,128)(2,1)} %get-tuple-element.30), calls=%async_computation.2 | async-start | bytes 524288 | tf_op jit(solution)/shard_map/all_to_all | solution.py:37
  192.0 15.5 %all-to-all-done.2.shares_ref = bf16[16,64,128]{2,1,0:T(8,128)(2,1)S(1)} async-done(((bf16[16,64,128]{2,1,0:T(8,128)(2,1)}), bf16[16,64,128]{2,1,0:T(8,128)(2,1)S(1)}, u32[]{:S(2)}, u32[]{:S(2)}) %all-to-all-start.2) | async-done | bytes 262176 | tf_op jit(solution)/shard_map/all_to_all | solution.py:37
  208.2 2.7 %grad_in_part.1 = bf16[4,848,128]{2,1,0:T(8,128)(2,1)} custom-call(bf16[16,64,128]{2,1,0:T(8,128)(2,1)} %copy-done.5, bf16[128,4096]{1,0:T(8,128)(2,1)} %bitcast.37, bf16[4,336,128]{2,1,0:T(8,128)(2,1)} %get-tuple-element.31.small_ref), custom_call_target="tpu_custom_call" | custom-call | tf_op jit(solution)/shard_map/grad_in_part/pallas_call | solution.py:398
  210.9 3.6 %all-to-all-start.3 = ((bf16[4,848,128]{2,1,0:T(8,128)(2,1)}), bf16[4,848,128]{2,1,0:T(8,128)(2,1)S(1)}, u32[]{:S(2)}, u32[]{:S(2)}) async-start(bf16[4,848,128]{2,1,0:T(8,128)(2,1)} %grad_in_part.1), calls=%async_computation.3 | async-start | bytes 1736704 | tf_op jit(solution)/shard_map/all_to_all | solution.py:37
  215.8 1.2 maximum_bitcast_fusion.scal_ref
  217.0 6.3 %all-to-all-done.3.got_ref = bf16[4,848,128]{2,1,0:T(8,128)(2,1)S(1)} async-done(((bf16[4,848,128]{2,1,0:T(8,128)(2,1)}), bf16[4,848,128]{2,1,0:T(8,128)(2,1)S(1)}, u32[]{:S(2)}, u32[]{:S(2)}) %all-to-all-start.3) | async-done | bytes 868384 | tf_op jit(solution)/shard_map/all_to_all | solution.py:37
  223.3 0.9 copy-done.4
  224.2 2.1 weigh.1
  226.3 13.0 %all-to-all-start.4 = ((bf16[8,112,128]{2,1,0:T(8,128)(2,1)}), bf16[8,112,128]{2,1,0:T(8,128)(2,1)S(1)}, u32[]{:S(2)}, u32[]{:S(2)}) async-start(bf16[8,112,128]{2,1,0:T(8,128)(2,1)} %weigh.1), calls=%async_computation.4 | async-start | bytes 458752 | tf_op jit(solution)/shard_map/all_to_all | solution.py:37
  239.3 6.2 %all-to-all-done.4 = bf16[8,112,128]{2,1,0:T(8,128)(2,1)S(1)} async-done(((bf16[8,112,128]{2,1,0:T(8,128)(2,1)}), bf16[8,112,128]{2,1,0:T(8,128)(2,1)S(1)}, u32[]{:S(2)}, u32[]{:S(2)}) %all-to-all-start.4) | async-done | bytes 229408 | tf_op jit(solution)/shard_map/all_to_all | solution.py:37
  246.0 20.8 %all_to_all.30 = bf16[16,16,128]{2,1,0:T(8,128)(2,1)S(1)} all-to-all(bf16[16,16,128]{2,1,0:T(8,128)(2,1)S(1)} %maximum_maximum_fusion), channel_id=1, replica_groups=mesh['zlo'=4,'x'=4,'core'=2,'y'=4,'zhi'=4] {'zlo','zhi'}, dimensions={0} | all-to-all | bytes 131072 | tf_op jit(solution)/shard_map/all_to_all | solution.py:37
  (60 shorter events, 7.4 us)
Async XLA Ops:
  7.1 15.8 %copy-start.7 = (bf16[1,128,64]{1,2,0:T(8,128)(2,1)S(1)}, bf16[1,128,64]{1,2,0:T(8,128)(2,1)}, u32[]{:S(2)}) copy-start(bf16[1,128,64]{1,2,0:T(8,128)(2,1)} %param.20) | copy-start | bytes 49156
  7.1 68.3 %all-to-all-start = ((bf16[4,1088,128]{2,1,0:T(8,128)(2,1)}), bf16[4,1088,128]{2,1,0:T(8,128)(2,1)S(1)}, u32[]{:S(2)}, u32[]{:S(2)}) async-start(bf16[4,1088,128]{2,1,0:T(8,128)(2,1)} %get-tuple-element.18), calls=%async_computation | async-start | bytes 2228224 | tf_op jit(solution)/shard_map/all_to_all | solution.py:37
  75.4 9.4 %copy-start = (bf16[4,1088,128]{2,1,0:T(8,128)(2,1)}, bf16[4,1088,128]{2,1,0:T(8,128)(2,1)S(1)}, u32[]{:S(2)}) copy-start(bf16[4,1088,128]{2,1,0:T(8,128)(2,1)S(1)} %all-to-all-done.refs_0_.refs_5_.refs_10_) | copy-start | bytes 3342340
  75.4 25.6 %collective-permute-start = (bf16[4,1088,128]{2,1,0:T(8,128)(2,1)S(1)}, bf16[4,1088,128]{2,1,0:T(8,128)(2,1)S(1)}, u32[]{:S(2)}, u32[]{:S(2)}) collective-permute-start(bf16[4,1088,128]{2,1,0:T(8,128)(2,1)S(1)} %all-to-all-done.refs_0_.refs_5_.refs_10_), channel_id=1, source_target_pairs={{0,12},{4,0},{8,4},{12,8},{1,13},{5,1},{9,5},{13,9},{2,14},{6,2},{... | collective-permute-start | bytes 3342344 | tf_op jit(solution)/shard_map/ppermute | solution.py:472
  80.0 27.2 %collective-permute-start.2 = (bf16[4,1088,128]{2,1,0:T(8,128)(2,1)S(1)}, bf16[4,1088,128]{2,1,0:T(8,128)(2,1)S(1)}, u32[]{:S(2)}, u32[]{:S(2)}) collective-permute-start(bf16[4,1088,128]{2,1,0:T(8,128)(2,1)S(1)} %all-to-all-done.refs_0_.refs_5_.refs_10_), channel_id=1, source_target_pairs={{0,4},{4,8},{8,12},{12,0},{1,5},{5,9},{9,13},{13,1},{2,6},{6,10},{... | collective-permute-start | bytes 3342344 | tf_op jit(solution)/shard_map/ppermute | solution.py:471
  82.8 9.2 %copy-start.8 = (s32[1,2048]{1,0:T(1,128)S(1)}, s32[1,2048]{1,0:T(1,128)}, u32[]{:S(2)}) copy-start(s32[1,2048]{1,0:T(1,128)} %param.17) | copy-start | bytes 24580
  84.8 30.2 %all-to-all-start.1 = ((bf16[4,576,128]{2,1,0:T(8,128)(2,1)}), bf16[4,576,128]{2,1,0:T(8,128)(2,1)}, u32[]{:S(2)}, u32[]{:S(2)}) async-start(bf16[4,576,128]{2,1,0:T(8,128)(2,1)} %pad_maximum_fusion.2), calls=%async_computation.1 | async-start | bytes 1179648 | tf_op jit(solution)/shard_map/all_to_all | solution.py:37
  100.9 12.0 %copy-start.1 = (bf16[4,1088,128]{2,1,0:T(8,128)(2,1)}, bf16[4,1088,128]{2,1,0:T(8,128)(2,1)S(1)}, u32[]{:S(2)}) copy-start(bf16[4,1088,128]{2,1,0:T(8,128)(2,1)S(1)} %collective-permute-done.refs_1_.refs_6_.refs_11_) | copy-start | bytes 3342340
  101.8 13.9 %collective-permute-start.1 = (bf16[2,1088,128]{2,1,0:T(8,128)(2,1)}, bf16[2,1088,128]{2,1,0:T(8,128)(2,1)}, u32[]{:S(2)}, u32[]{:S(2)}) collective-permute-start(bf16[2,1088,128]{2,1,0:T(8,128)(2,1)} %slice.41), channel_id=1, source_target_pairs={{0,12},{4,0},{8,4},{12,8},{1,13},{5,1},{9,5},{13,9},{2,14},{6,2},{... | collective-permute-start | bytes 1671176 | tf_op jit(solution)/shard_map/ppermute | solution.py:473
  107.3 5.7 %copy-start.2 = (bf16[4,1088,128]{2,1,0:T(8,128)(2,1)}, bf16[4,1088,128]{2,1,0:T(8,128)(2,1)S(1)}, u32[]{:S(2)}) copy-start(bf16[4,1088,128]{2,1,0:T(8,128)(2,1)S(1)} %collective-permute-done.2.refs_4_.refs_9_.refs_14_) | copy-start | bytes 3342340
  107.3 13.2 %collective-permute-start.3 = (bf16[2,1088,128]{2,1,0:T(8,128)(2,1)S(1)}, bf16[2,1088,128]{2,1,0:T(8,128)(2,1)S(1)}, u32[]{:S(2)}, u32[]{:S(2)}) collective-permute-start(bf16[2,1088,128]{2,1,0:T(8,128)(2,1)S(1)} %slice.42), channel_id=1, source_target_pairs={{0,4},{4,8},{8,12},{12,0},{1,5},{5,9},{9,13},{13,1},{2,6},{6,10},{... | collective-permute-start | bytes 1671176 | tf_op jit(solution)/shard_map/ppermute | solution.py:474
  120.5 0.8 copy-start.3
  185.5 22.0 %all-to-all-start.2 = ((bf16[16,64,128]{2,1,0:T(8,128)(2,1)}), bf16[16,64,128]{2,1,0:T(8,128)(2,1)S(1)}, u32[]{:S(2)}, u32[]{:S(2)}) async-start(bf16[16,64,128]{2,1,0:T(8,128)(2,1)} %get-tuple-element.30), calls=%async_computation.2 | async-start | bytes 524288 | tf_op jit(solution)/shard_map/all_to_all | solution.py:37
  207.5 0.7 copy-start.5
  210.9 3.8 %copy-start.9 = (s32[32]{0:T(128)S(1)}, s32[32]{0:T(128)}, u32[]{:S(2)}) copy-start(s32[32]{0:T(128)} %param.28) | copy-start | bytes 388
  210.9 3.8 %copy-start.10 = (f32[32]{0:T(128)S(1)}, f32[32]{0:T(128)}, u32[]{:S(2)}) copy-start(f32[32]{0:T(128)} %param.27) | copy-start | bytes 388
  210.9 12.4 %all-to-all-start.3 = ((bf16[4,848,128]{2,1,0:T(8,128)(2,1)}), bf16[4,848,128]{2,1,0:T(8,128)(2,1)S(1)}, u32[]{:S(2)}, u32[]{:S(2)}) async-start(bf16[4,848,128]{2,1,0:T(8,128)(2,1)} %grad_in_part.1), calls=%async_computation.3 | async-start | bytes 1736704 | tf_op jit(solution)/shard_map/all_to_all | solution.py:37
  217.0 51.0 %copy-start.6 = (bf16[256,128]{1,0:T(8,128)(2,1)S(1)}, bf16[256,128]{1,0:T(8,128)(2,1)}, u32[]{:S(2)}) copy-start(bf16[256,128]{1,0:T(8,128)(2,1)} %readout_ref.1) | copy-start | bytes 196612
  223.3 0.9 copy-start.4
  226.3 19.2 %all-to-all-start.4 = ((bf16[8,112,128]{2,1,0:T(8,128)(2,1)}), bf16[8,112,128]{2,1,0:T(8,128)(2,1)S(1)}, u32[]{:S(2)}, u32[]{:S(2)}) async-start(bf16[8,112,128]{2,1,0:T(8,128)(2,1)} %weigh.1), calls=%async_computation.4 | async-start | bytes 458752 | tf_op jit(solution)/shard_map/all_to_all | solution.py:37
